TPU v7x, 32 devices: a whole 2x2x4 slice. The times are simulated.
32 devices in a mesh: groups: 2 (over x), dp: 8 (over z, y), tensor: 2 (over core).
Axes of the slice: x: 2, y: 2, z: 4, core: 2. Of those that a mesh axis runs over, the one named last changes fastest.
Arguments:
- step_input: bfloat16 [1024, 4, 8192], P(('groups', 'dp'), None, 'tensor'), parts along dimension 0, may hold values from -8 to 8
- new_kv: bfloat16 [1024, 4, 2, 1024], P(('groups', 'dp'), None, None, 'tensor'), parts along dimension 0, may hold values from -24 to 24
- resp_cache: bfloat16 [1024, 8, 2, 1024], P(('groups', 'dp'), None, None, 'tensor'), parts along dimension 0, may hold values from -24 to 24
- policy_prompt: bfloat16 [16, 128, 2, 1024], P(('groups', 'dp'), None, None, 'tensor'), parts along dimension 0, may hold values from -24 to 24
- ref_prompt: bfloat16 [16, 128, 2, 1024], P(('groups', 'dp'), None, None, 'tensor'), parts along dimension 0, may hold values from -24 to 24
- prompt_len: int32 [16], P(('groups', 'dp')), parts along dimension 0, may hold values from 1 to 128
- resp_len: int32 [1024], P(('groups', 'dp')), parts along dimension 0, may hold values from 1 to 8
- row_owner: int32 [1024], P(('groups', 'dp')), parts along dimension 0, may hold values from 0 to 7, as said below
- finished: int32 [1024], P(('groups', 'dp')), parts along dimension 0, may hold values 0 or 1
- probe: float32 [8192], P('tensor'), may hold values from -0.12 to 0.12
Outputs:
- decoded: bfloat16 [1024, 4, 8192], P(('groups', 'dp'), None, 'tensor'), parts along dimension 0
- ref_score: float32 [16, 64, 4], P(('groups', 'dp')), parts along dimension 0
There are 2 independent parts, one for each index of `groups`. A program takes and returns all parts, laid end to end along the dimension named above; an argument that names none is the same for every part. Nothing has to cross between parts.
Inputs may be any that keep to these rules, and one draw needn't show every extreme that they name: `row_owner`: among the rows of one block at most 8 name the same owner; in every draw one owner is named by exactly 8 rows of every block.
All inputs are finite; a program needn't handle non-finite values. No bound on the sum of `finished` on one device may be relied on, other than what follows from the above.
Results may differ from a plain program's by a relative error of at most 0.012.
The roundings to bfloat16 on the way count: a program that leaves them out, or rounds other values in their place, can miss the bound.
Values may be sent and summed in bfloat16 or wider, within the bound.
A program may use at most 128 MiB of HBM per device.

v0:
```python
import functools
import math

import jax
import jax.numpy as jnp
from jax import lax
from jax.experimental import pallas as pl
from jax.experimental.pallas import tpu as pltpu
from jax.sharding import PartitionSpec as P

HD = 128
LOG2E = 1.4426950408889634


def softmax_pieces(scores, key_valid):
    masked = jnp.where(key_valid, scores, -jnp.inf)
    top_score = jnp.max(masked, axis=-1, keepdims=True)
    weight = jnp.exp(masked - top_score)
    return (weight, jnp.sum(weight, axis=-1), top_score[..., 0])


def per_device_routed(
    step_input,
    new_kv,
    resp_cache,
    policy_prompt,
    ref_prompt,
    prompt_len,
    resp_len,
    row_owner,
    finished,
    probe,
):
    row_count = step_input.shape[0]
    step_count = step_input.shape[1]
    q_width = step_input.shape[2]
    kv_width = new_kv.shape[3]
    q_heads = q_width // HD
    kv_heads = kv_width // HD
    group_size = q_heads // kv_heads
    inv_scale = 1.0 / math.sqrt(HD)
    peer_count = lax.axis_size("dp")
    capacity = max(2, (row_count + peer_count - 1) // peer_count)
    slot_count = peer_count * capacity
    resp_slots = resp_cache.shape[1]
    prompt_width = policy_prompt.shape[1]
    row_iota = jnp.arange(row_count, dtype=jnp.int32)
    same_owner = (row_owner[:, None] == row_owner[None, :]) & (
        row_iota[None, :] < row_iota[:, None]
    )
    slot_index = row_owner * capacity + jnp.sum(same_owner.astype(jnp.int32), axis=1)
    dispatch = slot_index[:, None] == jnp.arange(slot_count, dtype=jnp.int32)[None, :]
    one_hot = dispatch.T

    def to_slots(rows_data):
        picked = jnp.tensordot(one_hot.astype(rows_data.dtype), rows_data, axes=1)
        return picked.reshape((peer_count, capacity) + rows_data.shape[1:])

    live_len = jnp.where(finished == 1, resp_len, 0).astype(jnp.bfloat16)
    own_all = jnp.concatenate([resp_cache, new_kv], axis=1)
    reply_iota = jnp.arange(resp_slots + step_count)
    pol_keys = policy_prompt[0, :, 0].reshape(prompt_width, kv_heads, HD)
    pol_values = policy_prompt[0, :, 1].reshape(prompt_width, kv_heads, HD)
    prompt_valid = jnp.arange(prompt_width) < prompt_len[0]
    resp_keys = own_all[:, :, 0].reshape(row_count, -1, kv_heads, HD)
    resp_values = own_all[:, :, 1].reshape(row_count, -1, kv_heads, HD)
    previous = jnp.zeros((row_count, q_width), jnp.float32)
    decoded_list = []
    query_list = []
    kept_list = []
    for step_idx in range(step_count):
        queries = (step_input[:, step_idx].astype(jnp.float32) + previous).astype(jnp.bfloat16)
        query_list.append(queries)
        received = lax.all_to_all(to_slots(queries), "dp", split_axis=0, concat_axis=0, tiled=True)
        lead_shape = received.shape[:2]
        prompt_queries = received.reshape(-1, kv_heads, group_size, HD)
        scores = (
            jnp.einsum(
                "skgd,tkd->skgt", prompt_queries, pol_keys, preferred_element_type=jnp.float32
            )
            * inv_scale
        )
        prompt_weight, prompt_weight_sum, prompt_top_score = softmax_pieces(scores, prompt_valid)
        prompt_summed = jnp.einsum(
            "skgt,tkd->skgd",
            prompt_weight.astype(jnp.bfloat16),
            pol_values,
            preferred_element_type=jnp.float32,
        )
        part_out = (
            (prompt_summed / prompt_weight_sum[..., None])
            .astype(jnp.bfloat16)
            .reshape(lead_shape + (q_width,))
        )
        part_lse = (prompt_top_score + jnp.log(prompt_weight_sum)).reshape(lead_shape + (q_heads,))
        back_out = lax.all_to_all(part_out, "dp", split_axis=0, concat_axis=0, tiled=True)
        back_lse = lax.all_to_all(part_lse, "dp", split_axis=0, concat_axis=0, tiled=True)
        results = (back_out, back_lse, received)
        back_out = results[0]
        back_lse = results[1]
        kept_list.append(results[2])
        prompt_out = jnp.dot(
            dispatch.astype(jnp.bfloat16),
            back_out.reshape(slot_count, q_width),
            preferred_element_type=jnp.float32,
        )
        prompt_lse = jnp.dot(
            dispatch.astype(jnp.float32),
            back_lse.reshape(slot_count, q_heads),
            precision=lax.Precision.HIGHEST,
        )
        query_heads = queries.reshape(row_count, kv_heads, group_size, HD)
        scores = (
            jnp.einsum(
                "rkgd,rtkd->rkgt", query_heads, resp_keys, preferred_element_type=jnp.float32
            )
            * inv_scale
        )
        reply_valid = jnp.where(
            reply_iota[None, :] < resp_slots,
            reply_iota[None, :] < resp_len[:, None],
            reply_iota[None, :] <= resp_slots + step_idx,
        )
        weight, weight_sum, top_score = softmax_pieces(scores, reply_valid[:, None, None, :])
        summed = jnp.einsum(
            "rkgt,rtkd->rkgd",
            weight.astype(jnp.bfloat16),
            resp_values,
            preferred_element_type=jnp.float32,
        )
        own_out = (summed / weight_sum[..., None]).reshape(row_count, q_heads, HD)
        own_lse = (top_score + jnp.log(weight_sum)).reshape(row_count, q_heads)
        joint_lse = jnp.maximum(prompt_lse, own_lse)
        prompt_wt = jnp.exp(prompt_lse - joint_lse)
        own_wt = jnp.exp(own_lse - joint_lse)
        blended = (
            prompt_wt[..., None] * prompt_out.reshape(row_count, q_heads, HD)
            + own_wt[..., None] * own_out
        ) / (prompt_wt + own_wt)[..., None]
        decoded_now = blended.reshape(row_count, q_width).astype(jnp.bfloat16)
        decoded_list.append(decoded_now)
        previous = lax.optimization_barrier(decoded_now).astype(jnp.float32)
    recv_kv, recv_live = (
        lax.all_to_all(to_slots(own_all), "dp", split_axis=0, concat_axis=0, tiled=True),
        lax.all_to_all(to_slots(live_len), "dp", split_axis=0, concat_axis=0, tiled=True),
    )
    recv_queries = jnp.stack(kept_list, axis=2)
    ref_keys = ref_prompt[0, :, 0].reshape(prompt_width, kv_heads, HD)
    ref_values = ref_prompt[0, :, 1].reshape(prompt_width, kv_heads, HD)
    slot_kv = recv_kv.reshape(slot_count, resp_slots + step_count, 2, kv_width)
    slot_keys = slot_kv[:, :, 0].reshape(slot_count, -1, kv_heads, HD)
    slot_values = slot_kv[:, :, 1].reshape(slot_count, -1, kv_heads, HD)
    slot_len = recv_live.reshape(slot_count).astype(jnp.int32)
    slot_queries = recv_queries.reshape(slot_count, step_count, q_width)
    probe_heads = probe.reshape(kv_heads, group_size, HD)
    prompt_mask = jnp.broadcast_to(prompt_valid[None, :], (slot_count, prompt_width))
    score_list = []
    for step_idx in range(step_count):
        queries = slot_queries[:, step_idx].reshape(slot_count, kv_heads, group_size, HD)
        prompt_scores = (
            jnp.einsum("skgd,tkd->skgt", queries, ref_keys, preferred_element_type=jnp.float32)
            * inv_scale
        )
        reply_scores = (
            jnp.einsum("skgd,stkd->skgt", queries, slot_keys, preferred_element_type=jnp.float32)
            * inv_scale
        )
        reply_valid = jnp.where(
            reply_iota[None, :] < resp_slots,
            reply_iota[None, :] < slot_len[:, None],
            reply_iota[None, :] <= resp_slots + step_idx,
        )
        key_valid = jnp.concatenate([prompt_mask, reply_valid], axis=1)
        weight, weight_sum, top_score = softmax_pieces(
            jnp.concatenate([prompt_scores, reply_scores], axis=-1), key_valid[:, None, None, :]
        )
        weight_low = weight.astype(jnp.bfloat16)
        summed = jnp.einsum(
            "skgt,tkd->skgd",
            weight_low[..., :prompt_width],
            ref_values,
            preferred_element_type=jnp.float32,
        )
        summed = summed + jnp.einsum(
            "skgt,stkd->skgd",
            weight_low[..., prompt_width:],
            slot_values,
            preferred_element_type=jnp.float32,
        )
        ref_out = summed / weight_sum[..., None]
        score_list.append(
            jnp.einsum("skgd,kgd->s", ref_out, probe_heads, precision=lax.Precision.HIGHEST)
        )
    head_terms = jnp.stack(score_list, axis=1)
    head_total = lax.psum(head_terms, "tensor")
    ref_score = jnp.where(slot_len[:, None] > 0, head_total, jnp.zeros((), jnp.float32)).reshape(
        1, slot_count, step_count
    )
    return (jnp.stack(decoded_list, axis=1), ref_score)


def dot_t(a, b):
    return lax.dot_general(a, b, (((1,), (1,)), ((), ())), preferred_element_type=jnp.float32)


def dot_n(a, b):
    return lax.dot_general(a, b, (((1,), (0,)), ((), ())), preferred_element_type=jnp.float32)


def softmax_part(z, valid, values):
    masked = jnp.where(valid, z, -jnp.inf)
    top = jnp.max(masked, axis=-1, keepdims=True)
    weight = jnp.exp2(masked - top)
    total = jnp.sum(weight, axis=-1, keepdims=True)
    acc = dot_n(weight.astype(jnp.bfloat16), values)
    return top, total, acc


def owner_block(dims, prompt, x_at, kv_at, lens, probe, put_decoded):
    rows, step_count, resp_slots, width, kv_heads, group = dims
    keys_n = resp_slots + step_count
    qrows = group * rows
    scale = LOG2E / math.sqrt(HD)
    prompt_valid = prompt(4)[0:1, :width].astype(jnp.float32) > 0.5
    len_q = jnp.concatenate([lens] * group, axis=0)
    q_iota = lax.broadcasted_iota(jnp.int32, (qrows, keys_n * rows), 0)
    k_iota = lax.broadcasted_iota(jnp.int32, (qrows, keys_n * rows), 1)
    same_row = lax.rem(q_iota, rows) == lax.rem(k_iota, rows)
    key_t = lax.div(k_iota, rows)
    cached = same_row & (key_t < resp_slots) & (key_t < len_q)
    fresh = same_row & (key_t >= resp_slots)
    own_keys, own_values = [], []
    for k in range(kv_heads):
        own_keys.append(
            jnp.concatenate([kv_at(t, 0, k) for t in range(keys_n)], axis=0).astype(jnp.bfloat16)
        )
        own_values.append(
            jnp.concatenate([kv_at(t, 1, k) for t in range(keys_n)], axis=0).astype(jnp.bfloat16)
        )
    previous = [None] * kv_heads
    scores = []
    for s in range(step_count):
        own_valid = cached | (fresh & (key_t <= resp_slots + s))
        score = jnp.zeros((rows, HD), jnp.float32)
        for k in range(kv_heads):
            cols = slice(k * HD, (k + 1) * HD)
            q = jnp.concatenate([x_at(s, k * group + g) for g in range(group)], axis=0)
            if s > 0:
                q = q + previous[k]
            q = q.astype(jnp.bfloat16)
            top_p, sum_p, acc_p = softmax_part(
                dot_t(q, prompt(0)[:, cols]) * scale, prompt_valid, prompt(1)[:, cols]
            )
            top_o, sum_o, acc_o = softmax_part(
                dot_t(q, own_keys[k]) * scale, own_valid, own_values[k]
            )
            prompt_out = (acc_p / sum_p).astype(jnp.bfloat16).astype(jnp.float32)
            joint = jnp.maximum(top_p, top_o)
            wt_p = sum_p * jnp.exp2(top_p - joint)
            ex_o = jnp.exp2(top_o - joint)
            inv = 1.0 / (wt_p + ex_o * sum_o)
            decoded = (wt_p * inv) * prompt_out + (ex_o * inv) * acc_o
            decoded = decoded.astype(jnp.bfloat16).astype(jnp.float32)
            previous[k] = decoded
            put_decoded(s, k, decoded)
            top_r, sum_r, acc_r = softmax_part(
                dot_t(q, prompt(2)[:, cols]) * scale, prompt_valid, prompt(3)[:, cols]
            )
            joint = jnp.maximum(top_r, top_o)
            ex_r = jnp.exp2(top_r - joint)
            ex_o = jnp.exp2(top_o - joint)
            inv = 1.0 / (ex_r * sum_r + ex_o * sum_o)
            ref_out = (ex_r * inv) * acc_r + (ex_o * inv) * acc_o
            for g in range(group):
                h = k * group + g
                score = score + ref_out[g * rows : (g + 1) * rows] * probe[h : h + 1]
        scores.append(jnp.sum(score, axis=-1, keepdims=True))
    lane = lax.broadcasted_iota(jnp.int32, (rows, HD), 1)
    out = jnp.zeros((rows, HD), jnp.float32)
    for s in range(step_count):
        out = jnp.where(lane == s, scores[s], out)
    return out


def compute_kernel(dims, blk_ref, x_ref, kv_ref, len_ref, probe_ref, dec_ref, score_ref):
    rows, step_count, resp_slots, width, kv_heads, group = dims

    def prompt(part):
        if part == 4:
            return blk_ref[0, 4 * width :, :]
        return blk_ref[0, part * width : (part + 1) * width, :]

    def x_at(s, h):
        return x_ref[s, :, h * HD : (h + 1) * HD]

    def kv_at(t, c, k):
        return kv_ref[t, c, :, k * HD : (k + 1) * HD]

    def put_decoded(s, k, decoded):
        for g in range(group):
            h = k * group + g
            dec_ref[s, :, h * HD : (h + 1) * HD] = decoded[g * rows : (g + 1) * rows]

    score_ref[...] = owner_block(
        dims, prompt, x_at, kv_at, len_ref[:, 0:1], probe_ref[...], put_decoded
    )


def per_device_gathered(
    step_input,
    new_kv,
    resp_cache,
    policy_prompt,
    ref_prompt,
    prompt_len,
    resp_len,
    row_owner,
    finished,
    probe,
):
    row_count, step_count, q_width = step_input.shape
    kv_width = new_kv.shape[3]
    q_heads = q_width // HD
    kv_heads = kv_width // HD
    group = q_heads // kv_heads
    peers = lax.axis_size("dp")
    capacity = max(2, (row_count + peers - 1) // peers)
    slots = peers * capacity
    resp_slots = resp_cache.shape[1]
    keys_n = resp_slots + step_count
    width = policy_prompt.shape[1]
    mask = (jnp.arange(kv_width) < prompt_len[0]).astype(jnp.bfloat16)
    block = jnp.concatenate(
        [
            policy_prompt[0, :, 0],
            policy_prompt[0, :, 1],
            ref_prompt[0, :, 0],
            ref_prompt[0, :, 1],
            jnp.broadcast_to(mask[None, :], (16, kv_width)),
        ],
        axis=0,
    )
    blocks = lax.all_gather(block, "dp")
    iota = jnp.arange(row_count, dtype=jnp.int32)
    earlier = (row_owner[:, None] == row_owner[None, :]) & (iota[None, :] < iota[:, None])
    slot_index = row_owner * capacity + jnp.sum(earlier.astype(jnp.int32), axis=1)
    place = slot_index[None, :] == jnp.arange(slots, dtype=jnp.int32)[:, None]
    one_hot = place.astype(jnp.bfloat16)
    x_slots = jnp.einsum("pr,rse->spe", one_hot, step_input, preferred_element_type=jnp.float32)
    own_all = jnp.concatenate([resp_cache, new_kv], axis=1)
    kv_slots = jnp.einsum("pr,rtce->tcpe", one_hot, own_all, preferred_element_type=jnp.float32)
    len_slots = jnp.sum(jnp.where(place, resp_len[None, :], 0), axis=1)
    done_slots = jnp.sum(jnp.where(place, finished[None, :], 0), axis=1)
    dims = (capacity, step_count, resp_slots, width, kv_heads, group)
    decoded, scores = pl.pallas_call(
        functools.partial(compute_kernel, dims),
        grid=(peers,),
        in_specs=[
            pl.BlockSpec((1, block.shape[0], kv_width), lambda o: (o, 0, 0)),
            pl.BlockSpec((step_count, capacity, q_width), lambda o: (0, o, 0)),
            pl.BlockSpec((keys_n, 2, capacity, kv_width), lambda o: (0, 0, o, 0)),
            pl.BlockSpec((capacity, HD), lambda o: (o, 0)),
            pl.BlockSpec((q_heads, HD), lambda o: (0, 0)),
        ],
        out_specs=[
            pl.BlockSpec((step_count, capacity, q_width), lambda o: (0, o, 0)),
            pl.BlockSpec((capacity, HD), lambda o: (o, 0)),
        ],
        out_shape=[
            jax.ShapeDtypeStruct((step_count, slots, q_width), jnp.float32),
            jax.ShapeDtypeStruct((slots, HD), jnp.float32),
        ],
        compiler_params=pltpu.CompilerParams(vmem_limit_bytes=40 * 1024 * 1024),
    )(
        blocks,
        x_slots,
        kv_slots,
        jnp.broadcast_to(len_slots[:, None], (slots, HD)),
        probe.reshape(q_heads, HD),
    )
    decoded_rows = jnp.einsum(
        "pr,spe->rse",
        one_hot,
        decoded.astype(jnp.bfloat16),
        preferred_element_type=jnp.float32,
    ).astype(jnp.bfloat16)
    scores = jnp.where(done_slots[:, None] == 1, scores[:, :step_count], 0.0)
    scores = scores.reshape(peers, capacity, step_count)
    received = lax.all_to_all(scores, "dp", split_axis=0, concat_axis=0, tiled=True)
    total = lax.psum(received, "tensor")
    return decoded_rows, total.reshape(1, slots, step_count)


def per_device(step_input, *rest):
    peers = lax.axis_size("dp")
    rows = step_input.shape[0]
    if rows % (8 * peers) == 0:
        return per_device_gathered(step_input, *rest)
    return per_device_routed(step_input, *rest)


def solution(mesh):
    in_specs = (
        P(("groups", "dp"), None, "tensor"),
        P(("groups", "dp"), None, None, "tensor"),
        P(("groups", "dp"), None, None, "tensor"),
        P(("groups", "dp"), None, None, "tensor"),
        P(("groups", "dp"), None, None, "tensor"),
        P(("groups", "dp")),
        P(("groups", "dp")),
        P(("groups", "dp")),
        P(("groups", "dp")),
        P("tensor"),
    )
    out_specs = (P(("groups", "dp"), None, "tensor"), P(("groups", "dp"), None, None))
    return jax.shard_map(
        per_device, mesh=mesh, in_specs=in_specs, out_specs=out_specs, check_vma=False
    )
```

profile of v0, /device:TPU:0, one launch (start us, length us, event | category | flops | bytes accessed | tf_op | source)
XLA Modules:
  0.0 210.6 jit_solution(15721100775331262756)
XLA Ops:
  7.2 0.0 copy-start
  7.2 0.0 all-gather.3.cloned.1.call-start
  8.0 1.5 fusion.21
  9.5 0.0 copy-start.5
  9.5 1.6 fusion.20
  11.1 0.7 fusion.8
  11.8 0.7 fusion.7
  12.4 0.7 fusion.6
  13.1 0.0 copy-start.8
  13.1 0.0 copy-start.6
  13.1 0.0 copy-start.7
  13.1 0.7 fusion.5
  13.8 0.6 constant_dynamic-update-slice_fusion
  14.4 0.0 all-gather.3.cloned.1.call-update
  14.4 1.2 copy.63
  15.6 0.0 copy-done.5
  15.6 0.6 copy.62
  16.2 0.0 copy-done.8
  16.2 0.2 convert_reduce_fusion
  16.4 0.0 copy-done.6
  16.4 0.0 copy-done.7
  16.5 0.1 select_reduce_fusion
  16.6 2.5 %convolution_bitcast_fusion.1.kv_ref = f32[12,2,64,512]{3,2,1,0:T(8,128)} fusion(bf16[64,4,2,512]{3,0,2,1:T(8,128)(2,1)S(1)} %copy.63, bf16[64,8,2,512]{3,0,2,1:T(8,128)(2,1)S(1)} %copy.62, s32[64]{0:T(128)S(1)} %multiply_add_fusion), kind=kOutput, calls=%fused_computation.4 | convolution fusion | flops 101453824 | bytes 4718848 | tf_op jit(solution)/shard_map/pr,rtce->tcpe/dot_general | solution.py:351
  19.0 0.0 copy-done
  19.0 0.0 copy-start.4
  19.0 4.8 %convolution_bitcast_fusion.x_ref = f32[4,64,4096]{2,1,0:T(8,128)} fusion(bf16[64,4,4096]{2,1,0:T(4,128)(2,1)S(1)} %copy-done, s32[64]{0:T(128)S(1)} %multiply_add_fusion), kind=kOutput, calls=%fused_computation | convolution fusion | flops 134221824 | bytes 6291712 | tf_op jit(solution)/shard_map/pr,rse->spe/dot_general | solution.py:349
  23.8 68.4 %all-gather.3.cloned.1.call-done = bf16[4224,512]{1,0:T(8,128)(2,1)} async-done(((bf16[528,512]{1,0:T(8,128)(2,1)}), bf16[4224,512]{1,0:T(8,128)(2,1)}) %all-gather.3.cloned.1.call-update) | async-done | bytes 4325392 | tf_op jit(solution)/shard_map/all_gather | solution.py:343
  92.3 0.1 broadcast_in_dim.54.len_ref
  92.4 0.0 copy-done.4
  92.4 0.0 copy-start.1
  92.4 2.2 %copy-done.1 = f32[4,64,4096]{2,1,0:T(8,128)S(1)} copy-done((f32[4,64,4096]{2,1,0:T(8,128)S(1)}, f32[4,64,4096]{2,1,0:T(8,128)}, u32[]{:S(2)}) %copy-start.1) | copy-done | bytes 4194328
  94.6 0.0 copy-start.2
  94.6 1.9 copy-done.2
  96.5 91.6 %shard_map.113 = (f32[4,64,4096]{2,1,0:T(8,128)S(1)}, f32[64,128]{1,0:T(8,128)S(1)}) custom-call(bf16[8,528,512]{2,1,0:T(8,128)(2,1)} %bitcast.37, f32[4,64,4096]{2,1,0:T(8,128)S(1)} %copy-done.1, f32[12,2,64,512]{3,2,1,0:T(8,128)S(1)} %copy-done.2, s32[64,128]{1,0:T(8,128)S(1)} %broadcast_in_dim.54.len_ref, f32[32,128]{1,0:T(8,128)S(1)} %bitcast.36), custom_call_target="tpu_custom_call" | custom-call | tf_op jit(solution)/shard_map/pallas_call | solution.py:355
  188.1 0.0 copy-start.3
  188.1 1.9 copy-done.3
  190.0 0.1 select_bitcast_fusion
  190.1 0.7 copy.65
  190.8 3.3 %all-to-all-start = ((f32[8,8,4]{1,2,0:T(4,128)}), f32[8,8,4]{1,2,0:T(4,128)S(1)}, u32[]{:S(2)}, u32[]{:S(2)}) async-start(f32[8,8,4]{1,2,0:T(4,128)} %copy.65), calls=%async_computation | async-start | bytes 32768 | tf_op jit(solution)/shard_map/all_to_all | solution.py:389
  194.1 2.9 %convolution_convert_fusion = bf16[64,4,4096]{2,0,1:T(8,128)(2,1)S(1)} fusion(f32[4,64,4096]{2,1,0:T(8,128)} %copy-done.3, s32[64]{0:T(128)S(1)} %multiply_add_fusion), kind=kOutput, calls=%fused_computation.1 | convolution fusion | flops 136318976 | bytes 6291712 | tf_op jit(solution)/shard_map/pr,spe->rse/dot_general | solution.py:381
  197.1 2.9 %copy.67 = bf16[64,4,4096]{2,1,0:T(4,128)(2,1)} copy(bf16[64,4,4096]{2,0,1:T(8,128)(2,1)S(1)} %convolution_convert_fusion) | data formatting | bytes 4194304
  200.0 0.6 all-to-all-done
  200.6 0.1 reshape.30
  200.7 3.0 %psum.7 = f32[1,64,4]{1,2,0:T(4,128)} all-reduce(f32[1,64,4]{1,2,0:T(4,128)S(1)} %reshape.30), channel_id=1, replica_groups=mesh['groups'=2,'dp'=8,'tensor'=2] {'tensor'}, use_global_device_ids=true, to_apply=%region_3.4 | all-reduce | flops 256 | bytes 2048 | tf_op jit(solution)/shard_map/psum | solution.py:390
  (4 shorter events, 0.0 us)
Async XLA Ops:
  7.2 11.9 %copy-start = (bf16[64,4,4096]{2,1,0:T(4,128)(2,1)S(1)}, bf16[64,4,4096]{2,1,0:T(4,128)(2,1)}, u32[]{:S(2)}) copy-start(bf16[64,4,4096]{2,1,0:T(4,128)(2,1)} %param.10) | copy-start | bytes 6291460
  7.2 85.1 %all-gather.3.cloned.1.call-start = ((), (), s32[]{:S(2)}) async-start(), calls=%async_computation.1 | async-start | bytes 4866048 | tf_op jit(solution)/shard_map/all_gather | solution.py:343
  9.5 6.1 %copy-start.5 = (bf16[64,8,2,512]{3,2,1,0:T(2,128)(2,1)S(1)}, bf16[64,8,2,512]{3,2,1,0:T(2,128)(2,1)}, u32[]{:S(2)}) copy-start(bf16[64,8,2,512]{3,2,1,0:T(2,128)(2,1)} %param.12) | copy-start | bytes 3145732
  13.1 3.1 %copy-start.8 = (s32[64]{0:T(128)S(1)}, s32[64]{0:T(128)}, u32[]{:S(2)}) copy-start(s32[64]{0:T(128)} %param.17) | copy-start | bytes 772
  13.1 3.3 %copy-start.6 = (s32[64]{0:T(128)S(1)}, s32[64]{0:T(128)}, u32[]{:S(2)}) copy-start(s32[64]{0:T(128)} %param.18) | copy-start | bytes 772
  13.1 3.3 %copy-start.7 = (s32[64]{0:T(128)S(1)}, s32[64]{0:T(128)}, u32[]{:S(2)}) copy-start(s32[64]{0:T(128)} %param.16) | copy-start | bytes 772
  19.0 73.3 %copy-start.4 = (f32[4096]{0:T(1024)S(1)}, f32[4096]{0:T(1024)}, u32[]{:S(2)}) copy-start(f32[4096]{0:T(1024)} %param.19) | copy-start | bytes 49156
  92.4 2.2 %copy-start.1 = (f32[4,64,4096]{2,1,0:T(8,128)S(1)}, f32[4,64,4096]{2,1,0:T(8,128)}, u32[]{:S(2)}) copy-start(f32[4,64,4096]{2,1,0:T(8,128)} %convolution_bitcast_fusion.x_ref) | copy-start | bytes 12582916
  94.6 1.9 copy-start.2
  188.1 1.9 copy-start.3
  190.8 9.8 %all-to-all-start = ((f32[8,8,4]{1,2,0:T(4,128)}), f32[8,8,4]{1,2,0:T(4,128)S(1)}, u32[]{:S(2)}, u32[]{:S(2)}) async-start(f32[8,8,4]{1,2,0:T(4,128)} %copy.65), calls=%async_computation | async-start | bytes 32768 | tf_op jit(solution)/shard_map/all_to_all | solution.py:389
Sparse Core Ops, SparseCore 0:
  14.6 77.6 all-gather.2
where the time goes:
time: 211 us
  Pallas kernels  91.6 us (43%)
  waiting for transfers between devices  69.1 us (33%)
  local copies, waits for them, and re-layouts  18 us (9%)
  between operations  14.9 us (7%)
  matrix products  10.2 us (5%)
  starting transfers between devices  3.36 us (2%)
  blocking collectives  3.02 us (1%)
    pallas_call x1, Pallas kernels, per_device_gathered(): pl.pallas_call(functools.partial(compute_kernel, dims), grid=(peers,), in...  91.6 us
    all_gather x1, waiting for transfers between devices, per_device_gathered(): blocks = lax.all_gather(block, 'dp')  68.4 us
    unnamed x25, local copies, waits for them, and re-layouts  13.5 us
    dot_general x1, matrix products, per_device_gathered(): jnp.einsum('pr,rse->spe', one_hot, step_input, preferred_element_type=jnp...  4.8 us
  transfers between devices with their start and end apart: 2, of which 2 were waited for; matrix products, arithmetic and copies ran while one was open for 7% of the time, Pallas kernels for 0%

commit v1 on v0

--- a/solution.py
+++ b/solution.py
@@ -199,95 +199,100 @@
     return (jnp.stack(decoded_list, axis=1), ref_score)
 
 
-def dot_t(a, b):
-    return lax.dot_general(a, b, (((1,), (1,)), ((), ())), preferred_element_type=jnp.float32)
-
-
 def dot_n(a, b):
     return lax.dot_general(a, b, (((1,), (0,)), ((), ())), preferred_element_type=jnp.float32)
 
 
-def softmax_part(z, valid, values):
+def softmax_part(z, valid, both_heads, values_t):
     masked = jnp.where(valid, z, -jnp.inf)
-    top = jnp.max(masked, axis=-1, keepdims=True)
+    top = jnp.max(masked, axis=0, keepdims=True)
     weight = jnp.exp2(masked - top)
-    total = jnp.sum(weight, axis=-1, keepdims=True)
-    acc = dot_n(weight.astype(jnp.bfloat16), values)
+    total = jnp.sum(weight, axis=0, keepdims=True)
+    acc = dot_n(values_t, both_heads(weight.astype(jnp.bfloat16)))
     return top, total, acc
 
 
-def owner_block(dims, prompt, x_at, kv_at, lens, probe, put_decoded):
+def owner_block(dims, prompt, prompt_len, x_at, kv_at, lens, probe_at, put_decoded, put_score):
     rows, step_count, resp_slots, width, kv_heads, group = dims
     keys_n = resp_slots + step_count
-    qrows = group * rows
+    padded = HD // rows
+    lanes = 2 * group * rows
+    pairs = kv_heads // 2
     scale = LOG2E / math.sqrt(HD)
-    prompt_valid = prompt(4)[0:1, :width].astype(jnp.float32) > 0.5
-    len_q = jnp.concatenate([lens] * group, axis=0)
-    q_iota = lax.broadcasted_iota(jnp.int32, (qrows, keys_n * rows), 0)
-    k_iota = lax.broadcasted_iota(jnp.int32, (qrows, keys_n * rows), 1)
+    k_iota = lax.broadcasted_iota(jnp.int32, (HD, lanes), 0)
+    q_iota = lax.broadcasted_iota(jnp.int32, (HD, lanes), 1)
+    prompt_valid = k_iota.astype(jnp.float32) < prompt_len
     same_row = lax.rem(q_iota, rows) == lax.rem(k_iota, rows)
     key_t = lax.div(k_iota, rows)
-    cached = same_row & (key_t < resp_slots) & (key_t < len_q)
+    cached = same_row & (key_t < resp_slots) & (key_t < lens)
     fresh = same_row & (key_t >= resp_slots)
-    own_keys, own_values = [], []
-    for k in range(kv_heads):
-        own_keys.append(
-            jnp.concatenate([kv_at(t, 0, k) for t in range(keys_n)], axis=0).astype(jnp.bfloat16)
-        )
-        own_values.append(
-            jnp.concatenate([kv_at(t, 1, k) for t in range(keys_n)], axis=0).astype(jnp.bfloat16)
-        )
-    previous = [None] * kv_heads
-    scores = []
+    first = (q_iota < lanes // 2).astype(jnp.float32)
+    second = (1.0 - first).astype(jnp.bfloat16)
+    first = first.astype(jnp.bfloat16)
+
+    def both_heads(v):
+        return jnp.concatenate([v * first, v * second], axis=0)
+
+    blank = [jnp.zeros((rows, HD), jnp.float32)] * (padded - keys_n)
+
+    def stacked(c, k):
+        return jnp.concatenate([kv_at(t, c, k) for t in range(keys_n)] + blank, axis=0)
+
+    keys, own_values = [], []
+    for p in range(pairs):
+        cols = slice(2 * p * HD, 2 * (p + 1) * HD)
+        own = [stacked(0, 2 * p + i).astype(jnp.bfloat16) for i in range(2)]
+        keys.append(
+            jnp.concatenate(
+                [prompt(0)[:, cols], prompt(2)[:, cols], jnp.concatenate(own, axis=1)], axis=0
+            )
+        )
+        own = [stacked(1, 2 * p + i).T.astype(jnp.bfloat16) for i in range(2)]
+        own_values.append(jnp.concatenate(own, axis=1))
+    previous = [None] * pairs
     for s in range(step_count):
         own_valid = cached | (fresh & (key_t <= resp_slots + s))
-        score = jnp.zeros((rows, HD), jnp.float32)
-        for k in range(kv_heads):
-            cols = slice(k * HD, (k + 1) * HD)
-            q = jnp.concatenate([x_at(s, k * group + g) for g in range(group)], axis=0)
+        score = None
+        for p in range(pairs):
+            cols = slice(2 * p * HD, 2 * (p + 1) * HD)
+            heads = range(2 * p * group, 2 * (p + 1) * group)
+            q = jnp.concatenate([x_at(s, h) for h in heads], axis=0).T
             if s > 0:
-                q = q + previous[k]
-            q = q.astype(jnp.bfloat16)
+                q = q + previous[p]
+            z = dot_n(keys[p], both_heads(q.astype(jnp.bfloat16))) * scale
             top_p, sum_p, acc_p = softmax_part(
-                dot_t(q, prompt(0)[:, cols]) * scale, prompt_valid, prompt(1)[:, cols]
+                z[:width], prompt_valid, both_heads, prompt(1)[:, cols]
             )
             top_o, sum_o, acc_o = softmax_part(
-                dot_t(q, own_keys[k]) * scale, own_valid, own_values[k]
-            )
-            prompt_out = (acc_p / sum_p).astype(jnp.bfloat16).astype(jnp.float32)
+                z[2 * width :], own_valid, both_heads, own_values[p]
+            )
+            prompt_out = (acc_p * (1.0 / sum_p)).astype(jnp.bfloat16).astype(jnp.float32)
             joint = jnp.maximum(top_p, top_o)
             wt_p = sum_p * jnp.exp2(top_p - joint)
             ex_o = jnp.exp2(top_o - joint)
             inv = 1.0 / (wt_p + ex_o * sum_o)
             decoded = (wt_p * inv) * prompt_out + (ex_o * inv) * acc_o
             decoded = decoded.astype(jnp.bfloat16).astype(jnp.float32)
-            previous[k] = decoded
-            put_decoded(s, k, decoded)
+            previous[p] = decoded
+            put_decoded(s, p, decoded.T)
             top_r, sum_r, acc_r = softmax_part(
-                dot_t(q, prompt(2)[:, cols]) * scale, prompt_valid, prompt(3)[:, cols]
+                z[width : 2 * width], prompt_valid, both_heads, prompt(3)[:, cols]
             )
             joint = jnp.maximum(top_r, top_o)
             ex_r = jnp.exp2(top_r - joint)
             ex_o = jnp.exp2(top_o - joint)
             inv = 1.0 / (ex_r * sum_r + ex_o * sum_o)
-            ref_out = (ex_r * inv) * acc_r + (ex_o * inv) * acc_o
-            for g in range(group):
-                h = k * group + g
-                score = score + ref_out[g * rows : (g + 1) * rows] * probe[h : h + 1]
-        scores.append(jnp.sum(score, axis=-1, keepdims=True))
-    lane = lax.broadcasted_iota(jnp.int32, (rows, HD), 1)
-    out = jnp.zeros((rows, HD), jnp.float32)
-    for s in range(step_count):
-        out = jnp.where(lane == s, scores[s], out)
-    return out
+            probe = probe_at(p)
+            term = (ex_r * inv) * jnp.sum(acc_r * probe, axis=0, keepdims=True)
+            term = term + (ex_o * inv) * jnp.sum(acc_o * probe, axis=0, keepdims=True)
+            score = term if score is None else score + term
+        put_score(s, score)
 
 
 def compute_kernel(dims, blk_ref, x_ref, kv_ref, len_ref, probe_ref, dec_ref, score_ref):
     rows, step_count, resp_slots, width, kv_heads, group = dims
 
     def prompt(part):
-        if part == 4:
-            return blk_ref[0, 4 * width :, :]
         return blk_ref[0, part * width : (part + 1) * width, :]
 
     def x_at(s, h):
@@ -296,13 +301,25 @@
     def kv_at(t, c, k):
         return kv_ref[t, c, :, k * HD : (k + 1) * HD]
 
-    def put_decoded(s, k, decoded):
-        for g in range(group):
-            h = k * group + g
-            dec_ref[s, :, h * HD : (h + 1) * HD] = decoded[g * rows : (g + 1) * rows]
-
-    score_ref[...] = owner_block(
-        dims, prompt, x_at, kv_at, len_ref[:, 0:1], probe_ref[...], put_decoded
+    def put_decoded(s, p, decoded):
+        for i in range(2 * group):
+            h = 2 * p * group + i
+            dec_ref[s, :, h * HD : (h + 1) * HD] = decoded[i * rows : (i + 1) * rows]
+
+    def put_score(s, score):
+        score_ref[0, s : s + 1, :] = score
+
+    prompt_len = blk_ref[0, 4 * width :, :HD][0:1].astype(jnp.float32)
+    owner_block(
+        dims,
+        prompt,
+        prompt_len,
+        x_at,
+        kv_at,
+        len_ref[0, 0:1, :],
+        lambda p: probe_ref[p],
+        put_decoded,
+        put_score,
     )
 
 
@@ -329,14 +346,20 @@
     resp_slots = resp_cache.shape[1]
     keys_n = resp_slots + step_count
     width = policy_prompt.shape[1]
-    mask = (jnp.arange(kv_width) < prompt_len[0]).astype(jnp.bfloat16)
+    lanes = 2 * group * capacity
+    pairs = kv_heads // 2
+
+    def turned(values):
+        by_head = values.reshape(width, kv_heads, HD)
+        return jnp.transpose(by_head, (2, 1, 0)).reshape(HD, kv_heads * width)
+
     block = jnp.concatenate(
         [
             policy_prompt[0, :, 0],
-            policy_prompt[0, :, 1],
+            turned(policy_prompt[0, :, 1]),
             ref_prompt[0, :, 0],
-            ref_prompt[0, :, 1],
-            jnp.broadcast_to(mask[None, :], (16, kv_width)),
+            turned(ref_prompt[0, :, 1]),
+            jnp.broadcast_to(prompt_len.astype(jnp.bfloat16)[None, :], (16, kv_width)),
         ],
         axis=0,
     )
@@ -359,24 +382,28 @@
             pl.BlockSpec((1, block.shape[0], kv_width), lambda o: (o, 0, 0)),
             pl.BlockSpec((step_count, capacity, q_width), lambda o: (0, o, 0)),
             pl.BlockSpec((keys_n, 2, capacity, kv_width), lambda o: (0, 0, o, 0)),
-            pl.BlockSpec((capacity, HD), lambda o: (o, 0)),
-            pl.BlockSpec((q_heads, HD), lambda o: (0, 0)),
+            pl.BlockSpec((1, 8, lanes), lambda o: (o, 0, 0)),
+            pl.BlockSpec((pairs, HD, lanes), lambda o: (0, 0, 0)),
         ],
         out_specs=[
             pl.BlockSpec((step_count, capacity, q_width), lambda o: (0, o, 0)),
-            pl.BlockSpec((capacity, HD), lambda o: (o, 0)),
+            pl.BlockSpec((1, step_count, lanes), lambda o: (o, 0, 0)),
         ],
         out_shape=[
             jax.ShapeDtypeStruct((step_count, slots, q_width), jnp.float32),
-            jax.ShapeDtypeStruct((slots, HD), jnp.float32),
+            jax.ShapeDtypeStruct((peers, step_count, lanes), jnp.float32),
         ],
         compiler_params=pltpu.CompilerParams(vmem_limit_bytes=40 * 1024 * 1024),
     )(
         blocks,
         x_slots,
         kv_slots,
-        jnp.broadcast_to(len_slots[:, None], (slots, HD)),
-        probe.reshape(q_heads, HD),
+        jnp.broadcast_to(
+            len_slots.reshape(peers, 1, 1, capacity), (peers, 8, 2 * group, capacity)
+        ).reshape(peers, 8, lanes),
+        jnp.repeat(
+            jnp.transpose(probe.reshape(pairs, 2 * group, HD), (0, 2, 1)), capacity, axis=2
+        ),
     )
     decoded_rows = jnp.einsum(
         "pr,spe->rse",
@@ -384,8 +411,9 @@
         decoded.astype(jnp.bfloat16),
         preferred_element_type=jnp.float32,
     ).astype(jnp.bfloat16)
-    scores = jnp.where(done_slots[:, None] == 1, scores[:, :step_count], 0.0)
-    scores = scores.reshape(peers, capacity, step_count)
+    scores = scores.reshape(peers, step_count, 2 * group, capacity)
+    scores = jnp.transpose(jnp.sum(scores, axis=2), (0, 2, 1))
+    scores = jnp.where(done_slots.reshape(peers, capacity, 1) == 1, scores, 0.0)
     received = lax.all_to_all(scores, "dp", split_axis=0, concat_axis=0, tiled=True)
     total = lax.psum(received, "tensor")
     return decoded_rows, total.reshape(1, slots, step_count)
@@ -394,7 +422,16 @@
 def per_device(step_input, *rest):
     peers = lax.axis_size("dp")
     rows = step_input.shape[0]
-    if rows % (8 * peers) == 0:
+    step_count, q_width = step_input.shape[1:]
+    resp_slots, kv_width = rest[1].shape[1], rest[1].shape[3]
+    fits = (
+        rows == 8 * peers
+        and rest[2].shape[1] == HD
+        and 16 * q_width == HD * kv_width
+        and kv_width % (2 * HD) == 0
+        and 8 * (resp_slots + step_count) <= HD
+    )
+    if fits:
         return per_device_gathered(step_input, *rest)
     return per_device_routed(step_input, *rest)
 

time: 211 us -> 138 us (0.65)
  Pallas kernels: 91.6 us -> 19 us
  waiting for transfers between devices: 69.1 us -> 65.6 us
    pallas_call x1, Pallas kernels: 91.6 us -> 19 us  [per_device_gathered(): pl.pallas_call(functools.partial(compute_kernel, dims), grid=(peers,), in...]
    all_gather x1, waiting for transfers between devices: 68.4 us -> 65 us  [per_device_gathered(): blocks = lax.all_gather(block, 'dp')]
    unnamed x25 -> x28, local copies, waits for them, and re-layouts: 13.5 us -> 14.4 us
  transfers between devices with their start and end apart: 2 -> 2, of which waited for: 2 -> 2; matrix products, arithmetic and copies ran while one was open for 7% -> 14% of each run, Pallas kernels for 0% -> 0%
where the time goes in v1:
time: 138 us; the launch traced here: 137 us
  waiting for transfers between devices  65.6 us (48%)
  local copies, waits for them, and re-layouts  19.8 us (14%)
  Pallas kernels  19 us (14%)
  between operations  14.9 us (11%)
  matrix products  11.3 us (8%)
  starting transfers between devices  3.36 us (2%)
  blocking collectives  3.02 us (2%)
    all_gather x1, waiting for transfers between devices, per_device_gathered(): blocks = lax.all_gather(block, 'dp')  65 us
    pallas_call x1, Pallas kernels, per_device_gathered(): pl.pallas_call(functools.partial(compute_kernel, dims), grid=(peers,), in...  19 us
    unnamed x28, local copies, waits for them, and re-layouts  14.4 us
    dot_general x1, matrix products, per_device_gathered(): jnp.einsum('pr,rse->spe', one_hot, step_input, preferred_element_type=jnp...  4.8 us
    dot_general x1, matrix products, per_device_gathered(): jnp.einsum('pr,rtce->tcpe', one_hot, own_all, preferred_element_type=jnp....  3.56 us
    all_to_all x1, starting transfers between devices, per_device_gathered(): lax.all_to_all(scores, 'dp', split_axis=0, concat_axis=0, tiled=True)  3.33 us
    psum x1, blocking collectives, per_device_gathered(): total = lax.psum(received, 'tensor')  3.02 us
    dot_general x1, matrix products, per_device_gathered(): jnp.einsum('pr,spe->rse', one_hot, decoded.astype(jnp.bfloat16), preferre...  2.94 us
  transfers between devices with their start and end apart: 2, of which 2 were waited for; matrix products, arithmetic and copies ran while one was open for 14% of the time, Pallas kernels for 0%

profile of v1, /device:TPU:0, one launch (start us, length us, event | category | flops | bytes accessed | tf_op | source)
XLA Modules:
  0.0 137.3 jit_solution(8077970943144509566)
XLA Ops:
  7.2 0.0 copy-start
  7.2 0.0 copy-start.4
  7.2 0.0 all-gather.3.cloned.1.call-start
  7.2 1.7 %fusion.16 = (bf16[1,128,1,512]{3,2,1,0:T(2,128)(2,1)S(1)}, bf16[1,128,1,512]{3,2,1,0:T(2,128)(2,1)S(1)}) fusion(bf16[1,128,2,512]{3,2,1,0:T(2,128)(2,1)} %param.13), kind=kLoop, calls=%fused_computation.30 | loop fusion | bytes 524288 | tf_op jit(solution)/shard_map/slice | solution.py:359
  8.9 0.2 copy.123
  9.1 0.2 copy.124
  9.3 0.8 copy.103
  10.1 0.0 copy-done.4
  10.1 0.4 fusion.15
  10.4 0.0 copy-start.8
  10.4 0.0 copy-start.6
  10.5 0.0 copy-start.7
  10.5 0.2 copy.127
  10.7 0.2 copy.126
  10.8 0.1 copy.106
  11.6 0.9 constant_dynamic-update-slice_fusion.1
  12.7 1.0 copy.108
  13.7 0.0 copy-start.5
  13.7 0.0 all-gather.3.cloned.1.call-update
  13.8 0.0 copy-done.8
  13.8 0.2 convert_reduce_fusion
  14.0 0.0 copy-done.6
  14.0 0.0 copy-done.7
  14.0 0.1 select_reduce_fusion
  14.1 0.1 broadcast_in_dim.64
  14.2 0.1 broadcast_in_dim.66
  14.3 1.8 %copy.111 = bf16[64,8,2,512]{3,0,2,1:T(8,128)(2,1)S(1)} copy(bf16[64,8,2,512]{3,2,1,0:T(2,128)(2,1)} %param.12) | data formatting | bytes 2097152 | tf_op args[2]
  16.1 2.0 %copy.112 = bf16[64,4,2,512]{3,0,2,1:T(8,128)(2,1)} copy(bf16[64,4,2,512]{3,2,1,0:T(2,128)(2,1)} %param.11) | data formatting | bytes 1048576 | tf_op args[1]
  18.1 0.0 copy-done.5
  18.1 0.1 copy.114.probe_ref
  18.2 0.1 eq.45
  18.3 3.6 %convolution_bitcast_fusion.1.kv_ref = f32[12,2,64,512]{3,2,1,0:T(8,128)} fusion(bf16[64,4,2,512]{3,0,2,1:T(8,128)(2,1)} %copy.112, bf16[64,8,2,512]{3,0,2,1:T(8,128)(2,1)S(1)} %copy.111, s32[64]{0:T(128)S(1)} %multiply_add_fusion), kind=kOutput, calls=%fused_computation.4 | convolution fusion | flops 101453824 | bytes 4718848 | tf_op jit(solution)/shard_map/pr,rtce->tcpe/dot_general | solution.py:374
  21.9 0.0 copy-done
  21.9 4.8 %convolution_bitcast_fusion.x_ref = f32[4,64,4096]{2,1,0:T(8,128)} fusion(bf16[64,4,4096]{2,1,0:T(4,128)(2,1)S(1)} %copy-done, s32[64]{0:T(128)S(1)} %multiply_add_fusion), kind=kOutput, calls=%fused_computation | convolution fusion | flops 134221824 | bytes 6291712 | tf_op jit(solution)/shard_map/pr,rse->spe/dot_general | solution.py:372
  26.7 65.0 %all-gather.3.cloned.1.call-done = bf16[4224,512]{1,0:T(8,128)(2,1)} async-done(((bf16[528,512]{1,0:T(8,128)(2,1)}), bf16[4224,512]{1,0:T(8,128)(2,1)}) %all-gather.3.cloned.1.call-update) | async-done | bytes 4325392 | tf_op jit(solution)/shard_map/all_gather | solution.py:366
  91.6 0.0 copy-start.1
  91.6 2.2 %copy-done.1 = f32[4,64,4096]{2,1,0:T(8,128)S(1)} copy-done((f32[4,64,4096]{2,1,0:T(8,128)S(1)}, f32[4,64,4096]{2,1,0:T(8,128)}, u32[]{:S(2)}) %copy-start.1) | copy-done | bytes 4194328
  93.8 0.0 copy-start.2
  93.8 1.9 %copy-done.2 = f32[12,2,64,512]{3,2,1,0:T(8,128)S(1)} copy-done((f32[12,2,64,512]{3,2,1,0:T(8,128)S(1)}, f32[12,2,64,512]{3,2,1,0:T(8,128)}, u32[]{:S(2)}) %copy-start.2) | copy-done | bytes 3145752
  95.7 19.0 %shard_map.113 = (f32[4,64,4096]{2,1,0:T(8,128)S(1)}, f32[8,4,128]{2,1,0:T(4,128)S(1)}) custom-call(bf16[8,528,512]{2,1,0:T(8,128)(2,1)} %bitcast.38, f32[4,64,4096]{2,1,0:T(8,128)S(1)} %copy-done.1, f32[12,2,64,512]{3,2,1,0:T(8,128)S(1)} %copy-done.2, s32[8,8,128]{2,1,0:T(8,128)S(1)} %broadcast_in_dim.67.len_ref, f32[2,128,128]{2,1,0:T(8,128)S(1)} %copy.114.probe_ref), custom_call_target="tpu_custom_call" | custom-call | tf_op jit(solution)/shard_map/pallas_call | solution.py:378
  114.7 0.0 copy-start.3
  114.7 1.9 %copy-done.3 = f32[4,64,4096]{2,1,0:T(8,128)} copy-done((f32[4,64,4096]{2,1,0:T(8,128)}, f32[4,64,4096]{2,1,0:T(8,128)S(1)}, u32[]{:S(2)}) %copy-start.3) | copy-done | bytes 4194328
  116.6 0.2 reshape.46
  116.9 0.6 copy.116
  117.5 3.3 %all-to-all-start = ((f32[8,8,4]{1,2,0:T(4,128)}), f32[8,8,4]{1,2,0:T(4,128)S(1)}, u32[]{:S(2)}, u32[]{:S(2)}) async-start(f32[8,8,4]{1,2,0:T(4,128)} %copy.116), calls=%async_computation | async-start | bytes 32768 | tf_op jit(solution)/shard_map/all_to_all | solution.py:417
  120.8 2.9 %convolution_convert_fusion = bf16[64,4,4096]{2,0,1:T(8,128)(2,1)S(1)} fusion(f32[4,64,4096]{2,1,0:T(8,128)} %copy-done.3, s32[64]{0:T(128)S(1)} %multiply_add_fusion), kind=kOutput, calls=%fused_computation.1 | convolution fusion | flops 136318976 | bytes 6291712 | tf_op jit(solution)/shard_map/pr,spe->rse/dot_general | solution.py:408
  123.8 2.9 %copy.118 = bf16[64,4,4096]{2,1,0:T(4,128)(2,1)} copy(bf16[64,4,4096]{2,0,1:T(8,128)(2,1)S(1)} %convolution_convert_fusion) | data formatting | bytes 4194304
  126.7 0.6 all-to-all-done
  127.3 0.1 reshape.47
  127.4 3.0 %psum.7 = f32[1,64,4]{1,2,0:T(4,128)} all-reduce(f32[1,64,4]{1,2,0:T(4,128)S(1)} %reshape.47), channel_id=1, replica_groups=mesh['groups'=2,'dp'=8,'tensor'=2] {'tensor'}, use_global_device_ids=true, to_apply=%region_4.5 | all-reduce | flops 256 | bytes 2048 | tf_op jit(solution)/shard_map/psum | solution.py:418
  (13 shorter events, 0.2 us)
Async XLA Ops:
  7.2 14.7 %copy-start = (bf16[64,4,4096]{2,1,0:T(4,128)(2,1)S(1)}, bf16[64,4,4096]{2,1,0:T(4,128)(2,1)}, u32[]{:S(2)}) copy-start(bf16[64,4,4096]{2,1,0:T(4,128)(2,1)} %param.10) | copy-start | bytes 6291460
  7.2 2.9 %copy-start.4 = (bf16[1,128,2,512]{3,2,1,0:T(2,128)(2,1)S(1)}, bf16[1,128,2,512]{3,2,1,0:T(2,128)(2,1)}, u32[]{:S(2)}) copy-start(bf16[1,128,2,512]{3,2,1,0:T(2,128)(2,1)} %param.14) | copy-start | bytes 786436
  7.2 84.4 %all-gather.3.cloned.1.call-start = ((), (), s32[]{:S(2)}) async-start(), calls=%async_computation.1 | async-start | bytes 4866048 | tf_op jit(solution)/shard_map/all_gather | solution.py:366
  10.4 3.3 %copy-start.8 = (s32[64]{0:T(128)S(1)}, s32[64]{0:T(128)}, u32[]{:S(2)}) copy-start(s32[64]{0:T(128)} %param.17) | copy-start | bytes 772
  10.4 3.5 %copy-start.6 = (s32[64]{0:T(128)S(1)}, s32[64]{0:T(128)}, u32[]{:S(2)}) copy-start(s32[64]{0:T(128)} %param.18) | copy-start | bytes 772
  10.5 3.5 %copy-start.7 = (s32[64]{0:T(128)S(1)}, s32[64]{0:T(128)}, u32[]{:S(2)}) copy-start(s32[64]{0:T(128)} %param.16) | copy-start | bytes 772
  13.7 4.3 %copy-start.5 = (f32[4096]{0:T(1024)S(1)}, f32[4096]{0:T(1024)}, u32[]{:S(2)}) copy-start(f32[4096]{0:T(1024)} %param.19) | copy-start | bytes 49156
  91.6 2.2 %copy-start.1 = (f32[4,64,4096]{2,1,0:T(8,128)S(1)}, f32[4,64,4096]{2,1,0:T(8,128)}, u32[]{:S(2)}) copy-start(f32[4,64,4096]{2,1,0:T(8,128)} %convolution_bitcast_fusion.x_ref) | copy-start | bytes 12582916
  93.8 1.9 %copy-start.2 = (f32[12,2,64,512]{3,2,1,0:T(8,128)S(1)}, f32[12,2,64,512]{3,2,1,0:T(8,128)}, u32[]{:S(2)}) copy-start(f32[12,2,64,512]{3,2,1,0:T(8,128)} %convolution_bitcast_fusion.1.kv_ref) | copy-start | bytes 9437188
  114.7 1.9 %copy-start.3 = (f32[4,64,4096]{2,1,0:T(8,128)}, f32[4,64,4096]{2,1,0:T(8,128)S(1)}, u32[]{:S(2)}) copy-start(f32[4,64,4096]{2,1,0:T(8,128)S(1)} %get-tuple-element.4) | copy-start | bytes 12582916
  117.5 9.8 %all-to-all-start = ((f32[8,8,4]{1,2,0:T(4,128)}), f32[8,8,4]{1,2,0:T(4,128)S(1)}, u32[]{:S(2)}, u32[]{:S(2)}) async-start(f32[8,8,4]{1,2,0:T(4,128)} %copy.116), calls=%async_computation | async-start | bytes 32768 | tf_op jit(solution)/shard_map/all_to_all | solution.py:417
Sparse Core Ops, SparseCore 0:
  13.9 77.6 all-gather.2

commit v2 on v1

--- a/solution.py
+++ b/solution.py
@@ -289,38 +289,176 @@
         put_score(s, score)
 
 
-def compute_kernel(dims, blk_ref, x_ref, kv_ref, len_ref, probe_ref, dec_ref, score_ref):
+def fused_kernel(
+    dims,
+    blk_ref,
+    x_ref,
+    kv_ref,
+    len_ref,
+    done_ref,
+    probe_ref,
+    dec_ref,
+    score_ref,
+    buf,
+    mail,
+    got,
+    own_sem,
+    send_sem,
+    recv_sem,
+    mail_send,
+    mail_recv,
+):
     rows, step_count, resp_slots, width, kv_heads, group = dims
-
-    def prompt(part):
-        return blk_ref[0, part * width : (part + 1) * width, :]
-
-    def x_at(s, h):
-        return x_ref[s, :, h * HD : (h + 1) * HD]
-
-    def kv_at(t, c, k):
-        return kv_ref[t, c, :, k * HD : (k + 1) * HD]
-
-    def put_decoded(s, p, decoded):
-        for i in range(2 * group):
-            h = 2 * p * group + i
-            dec_ref[s, :, h * HD : (h + 1) * HD] = decoded[i * rows : (i + 1) * rows]
-
-    def put_score(s, score):
-        score_ref[0, s : s + 1, :] = score
-
-    prompt_len = blk_ref[0, 4 * width :, :HD][0:1].astype(jnp.float32)
-    owner_block(
-        dims,
-        prompt,
-        prompt_len,
-        x_at,
-        kv_at,
-        len_ref[0, 0:1, :],
-        lambda p: probe_ref[p],
-        put_decoded,
-        put_score,
-    )
+    n = buf.shape[0]
+    half = n // 2
+    tensors = got.shape[0]
+    part = lax.axis_index("groups")
+    me = lax.axis_index("dp")
+    tau = lax.axis_index("tensor")
+    z = lax.div(me, 2)
+    y = lax.rem(me, 2)
+
+    def device(dp, t):
+        return (part, dp, t)
+
+    barrier = pltpu.get_barrier_semaphore()
+    for dt in range(tensors):
+        for j in range(n):
+            if dt or j:
+                pl.semaphore_signal(
+                    barrier,
+                    inc=1,
+                    device_id=device(lax.rem(me + j, n), lax.rem(tau + dt, tensors)),
+                    device_id_type=pl.DeviceIdType.MESH,
+                )
+    pl.semaphore_wait(barrier, tensors * n - 1)
+
+    across = me + 1 - 2 * y
+    targets = (jnp.minimum(me + 2, n - 2 + y), jnp.maximum(me - 2, y), across)
+
+    def hop(src, o, way):
+        return pltpu.make_async_remote_copy(
+            src_ref=src,
+            dst_ref=buf.at[o],
+            send_sem=send_sem.at[way, o],
+            recv_sem=recv_sem.at[o],
+            device_id=device(targets[way], tau),
+            device_id_type=pl.DeviceIdType.MESH,
+        )
+
+    def each_way(zz, act):
+        o = 2 * zz + y
+        pl.when((z < half - 1) & (zz <= z))(lambda: act(o, 0))
+        pl.when((z > 0) & (zz >= z))(lambda: act(o, 1))
+        act(o, 2)
+
+    each_way(z, lambda o, way: hop(blk_ref, o, way).start())
+    own = pltpu.make_async_copy(blk_ref, buf.at[me], own_sem)
+    own.start()
+    own.wait()
+
+    def by_distance(i):
+        up, down = half - 1 - z, z
+        near = jnp.minimum(up, down)
+        paired = lax.div(i + 1, 2) * jnp.where(lax.rem(i, 2) == 1, 1, -1)
+        beyond = (i - near) * jnp.where(up > down, 1, -1)
+        return z + jnp.where(i <= 2 * near, paired, beyond)
+
+    def letter(o, dt):
+        return pltpu.make_async_remote_copy(
+            src_ref=mail.at[o],
+            dst_ref=got.at[tau, me],
+            send_sem=mail_send.at[dt, o],
+            recv_sem=mail_recv.at[tau, me],
+            device_id=device(o, lax.rem(tau + dt, tensors)),
+            device_id_type=pl.DeviceIdType.MESH,
+        )
+
+    def turn(t, carry):
+        odd = lax.rem(t, 2) == 1
+        last = t == n - 1
+        line = (t == 0) | (odd & jnp.logical_not(last))
+        order = jnp.where(
+            line, lax.div(t + 1, 2), jnp.where(last, half - 1, lax.div(t, 2) - 1)
+        )
+        zz = by_distance(order)
+        o = 2 * zz + jnp.where(line, y, 1 - y)
+
+        @pl.when(t > 0)
+        def _():
+            hop(buf.at[o], o, 2).wait_recv()
+
+        @pl.when((t > 0) & line)
+        def _():
+            each_way(zz, lambda b, way: hop(buf.at[b], b, way).start())
+
+        here = pl.ds(pl.multiple_of(o * rows, rows), rows)
+
+        def put_decoded(s, p, decoded):
+            for i in range(2 * group):
+                h = 2 * p * group + i
+                dec_ref[s, here, h * HD : (h + 1) * HD] = decoded[i * rows : (i + 1) * rows]
+
+        def put_score(s, score):
+            mail[o, s : s + 1, :] = jnp.where(done_ref[o, 0:1, :] == 1, score, 0.0)
+
+        owner_block(
+            dims,
+            lambda i: buf[o, i * width : (i + 1) * width, :],
+            buf[o, 4 * width :, :HD][0:1].astype(jnp.float32),
+            lambda s, h: x_ref[s, here, h * HD : (h + 1) * HD],
+            lambda t, c, k: kv_ref[t, c, here, k * HD : (k + 1) * HD],
+            len_ref[o, 0:1, :],
+            lambda p: probe_ref[p],
+            put_decoded,
+            put_score,
+        )
+        for dt in range(1, tensors):
+            letter(o, dt).start()
+        pl.when(o != me)(lambda: letter(o, 0).start())
+
+        @pl.when(o == me)
+        def _():
+            got[tau, me] = mail[me]
+
+        return carry
+
+    mail[...] = jnp.zeros_like(mail)
+    lax.fori_loop(0, n, turn, 0)
+
+    def arrived(t, b):
+        return pltpu.make_async_remote_copy(
+            src_ref=mail.at[b],
+            dst_ref=got.at[t, b],
+            send_sem=mail_send.at[0, b],
+            recv_sem=mail_recv.at[t, b],
+            device_id=device(across, tau),
+            device_id_type=pl.DeviceIdType.MESH,
+        )
+
+    def finish(b, carry):
+        for dt in range(1, tensors):
+            arrived(lax.rem(tau + dt, tensors), b).wait_recv()
+            letter(b, dt).wait_send()
+
+        @pl.when(b != me)
+        def _():
+            arrived(tau, b).wait_recv()
+            letter(b, 0).wait_send()
+
+        return carry
+
+    lax.fori_loop(0, n, finish, 0)
+
+    def sent(zz, carry):
+        each_way(zz, lambda o, way: hop(buf.at[o], o, way).wait_send())
+        return carry
+
+    lax.fori_loop(0, half, sent, 0)
+    total = got[0]
+    for t in range(1, tensors):
+        total = total + got[t]
+    score_ref[...] = total
 
 
 def per_device_gathered(
@@ -363,7 +501,6 @@
         ],
         axis=0,
     )
-    blocks = lax.all_gather(block, "dp")
     iota = jnp.arange(row_count, dtype=jnp.int32)
     earlier = (row_owner[:, None] == row_owner[None, :]) & (iota[None, :] < iota[:, None])
     slot_index = row_owner * capacity + jnp.sum(earlier.astype(jnp.int32), axis=1)
@@ -375,32 +512,42 @@
     len_slots = jnp.sum(jnp.where(place, resp_len[None, :], 0), axis=1)
     done_slots = jnp.sum(jnp.where(place, finished[None, :], 0), axis=1)
     dims = (capacity, step_count, resp_slots, width, kv_heads, group)
+
+    def on_lanes(values):
+        by_slot = values.reshape(peers, 1, 1, capacity)
+        return jnp.broadcast_to(by_slot, (peers, 8, 2 * group, capacity)).reshape(
+            peers, 8, lanes
+        )
+
+    tensors = lax.axis_size("tensor")
+    vmem = pl.BlockSpec(memory_space=pltpu.VMEM)
     decoded, scores = pl.pallas_call(
-        functools.partial(compute_kernel, dims),
-        grid=(peers,),
-        in_specs=[
-            pl.BlockSpec((1, block.shape[0], kv_width), lambda o: (o, 0, 0)),
-            pl.BlockSpec((step_count, capacity, q_width), lambda o: (0, o, 0)),
-            pl.BlockSpec((keys_n, 2, capacity, kv_width), lambda o: (0, 0, o, 0)),
-            pl.BlockSpec((1, 8, lanes), lambda o: (o, 0, 0)),
-            pl.BlockSpec((pairs, HD, lanes), lambda o: (0, 0, 0)),
-        ],
-        out_specs=[
-            pl.BlockSpec((step_count, capacity, q_width), lambda o: (0, o, 0)),
-            pl.BlockSpec((1, step_count, lanes), lambda o: (o, 0, 0)),
-        ],
+        functools.partial(fused_kernel, dims),
+        in_specs=[vmem] * 6,
+        out_specs=[vmem] * 2,
         out_shape=[
             jax.ShapeDtypeStruct((step_count, slots, q_width), jnp.float32),
-            jax.ShapeDtypeStruct((peers, step_count, lanes), jnp.float32),
+            jax.ShapeDtypeStruct((peers, 8, lanes), jnp.float32),
         ],
-        compiler_params=pltpu.CompilerParams(vmem_limit_bytes=40 * 1024 * 1024),
+        scratch_shapes=[
+            pltpu.VMEM((peers,) + block.shape, jnp.bfloat16),
+            pltpu.VMEM((peers, 8, lanes), jnp.float32),
+            pltpu.VMEM((tensors, peers, 8, lanes), jnp.float32),
+            pltpu.SemaphoreType.DMA,
+            pltpu.SemaphoreType.DMA((3, peers)),
+            pltpu.SemaphoreType.DMA((peers,)),
+            pltpu.SemaphoreType.DMA((tensors, peers)),
+            pltpu.SemaphoreType.DMA((tensors, peers)),
+        ],
+        compiler_params=pltpu.CompilerParams(
+            collective_id=0, has_side_effects=True, vmem_limit_bytes=48 * 1024 * 1024
+        ),
     )(
-        blocks,
+        block,
         x_slots,
         kv_slots,
-        jnp.broadcast_to(
-            len_slots.reshape(peers, 1, 1, capacity), (peers, 8, 2 * group, capacity)
-        ).reshape(peers, 8, lanes),
+        on_lanes(len_slots),
+        on_lanes(done_slots),
         jnp.repeat(
             jnp.transpose(probe.reshape(pairs, 2 * group, HD), (0, 2, 1)), capacity, axis=2
         ),
@@ -411,12 +558,9 @@
         decoded.astype(jnp.bfloat16),
         preferred_element_type=jnp.float32,
     ).astype(jnp.bfloat16)
-    scores = scores.reshape(peers, step_count, 2 * group, capacity)
+    scores = scores[:, :step_count].reshape(peers, step_count, 2 * group, capacity)
     scores = jnp.transpose(jnp.sum(scores, axis=2), (0, 2, 1))
-    scores = jnp.where(done_slots.reshape(peers, capacity, 1) == 1, scores, 0.0)
-    received = lax.all_to_all(scores, "dp", split_axis=0, concat_axis=0, tiled=True)
-    total = lax.psum(received, "tensor")
-    return decoded_rows, total.reshape(1, slots, step_count)
+    return decoded_rows, scores.reshape(1, slots, step_count)
 
 
 def per_device(step_input, *rest):
@@ -430,6 +574,8 @@
         and 16 * q_width == HD * kv_width
         and kv_width % (2 * HD) == 0
         and 8 * (resp_slots + step_count) <= HD
+        and peers % 2 == 0
+        and step_count <= 8
     )
     if fits:
         return per_device_gathered(step_input, *rest)

time: 138 us -> 98.1 us (0.71)
  waiting for transfers between devices: 65.6 us -> 0 us
  Pallas kernels: 19 us -> 71.7 us
  between operations: 14.9 us -> 1.63 us
  local copies, waits for them, and re-layouts: 19.8 us -> 13.4 us
  starting transfers between devices: 3.36 us -> 0 us
  blocking collectives: 3.02 us -> 0 us
  matrix products: 11.3 us -> 8.45 us
  other arithmetic: 0.35 us -> 2.4 us
    all_gather x1 -> x0, waiting for transfers between devices: 65 us -> none  [per_device_gathered(): blocks = lax.all_gather(block, 'dp')]
    pallas_call x1, Pallas kernels: 19 us -> 71.7 us  [per_device_gathered(): pl.pallas_call(functools.partial(fused_kernel, dims), in_specs=[vmem] * 6...]
    unnamed x28 -> x15, local copies, waits for them, and re-layouts: 14.4 us -> 9.2 us
    all_to_all x1 -> x0, starting transfers between devices: 3.33 us -> none  [per_device_gathered(): lax.all_to_all(scores, 'dp', split_axis=0, concat_axis=0, tiled=True)]
    psum x1 -> x0, blocking collectives: 3.02 us -> none  [per_device_gathered(): total = lax.psum(received, 'tensor')]
    dot_general x1, matrix products: 3.56 us -> 0.76 us  [per_device_gathered(): jnp.einsum('pr,rtce->tcpe', one_hot, own_all, preferred_element_type=jnp....]
  transfers between devices with their start and end apart: 2 -> 0, of which waited for: 2 -> 0; matrix products, arithmetic and copies ran while one was open for 14% -> 0% of each run, Pallas kernels for 0% -> 0%
where the time goes in v2:
time: 98.1 us; the launch traced here: 97.6 us
  Pallas kernels  71.7 us (73%)
  local copies, waits for them, and re-layouts  13.4 us (14%)
  matrix products  8.45 us (9%)
  other arithmetic  2.4 us (2%)
  between operations  1.63 us (2%)
    pallas_call x1, Pallas kernels, per_device_gathered(): pl.pallas_call(functools.partial(fused_kernel, dims), in_specs=[vmem] * 6...  71.7 us
    unnamed x15, local copies, waits for them, and re-layouts  9.2 us
    dot_general x1, matrix products, per_device_gathered(): jnp.einsum('pr,rse->spe', one_hot, step_input, preferred_element_type=jnp...  4.76 us
    dot_general x1, matrix products, per_device_gathered(): jnp.einsum('pr,spe->rse', one_hot, decoded.astype(jnp.bfloat16), preferre...  2.93 us

profile of v2, /device:TPU:0, one launch (start us, length us, event | category | flops | bytes accessed | tf_op | source)
XLA Modules:
  0.0 97.6 jit_solution(16270293828274217594)
XLA Ops:
  0.6 0.0 copy-start
  0.6 0.0 copy-start.2
  0.7 0.0 copy-start.1
  1.5 0.9 convert_reduce_fusion
  2.4 0.7 multiply_add_fusion
  3.1 0.8 select_reduce_fusion
  3.8 0.1 broadcast_in_dim.68
  3.9 0.1 broadcast_in_dim.63
  4.0 0.1 broadcast_in_dim.65
  4.1 0.1 broadcast_in_dim.70
  4.2 0.7 broadcast_bitcast_fusion
  5.0 0.1 copy.47.probe_ref
  5.1 1.2 %copy.45 = bf16[64,4,2,512]{3,0,2,1:T(8,128)(2,1)S(1)} copy(bf16[64,4,2,512]{3,2,1,0:T(2,128)(2,1)} %param.11) | data formatting | bytes 1048576 | tf_op args[1]
  6.3 0.0 copy-done.1
  6.3 1.2 %fusion.18 = (bf16[1,128,1,512]{3,2,1,0:T(2,128)(2,1)}, bf16[1,128,1,512]{3,2,1,0:T(2,128)(2,1)}) fusion(bf16[1,128,2,512]{3,2,1,0:T(2,128)(2,1)S(1)} %copy-done.1), kind=kLoop, calls=%fused_computation.30 | loop fusion | bytes 524288 | tf_op jit(solution)/shard_map/slice | solution.py:497
  7.4 1.1 %copy.55 = bf16[1,128,1,512]{1,3,2,0:T(8,128)(2,1)S(1)} copy(bf16[1,128,1,512]{3,2,1,0:T(2,128)(2,1)} %get-tuple-element.16) | data formatting | bytes 262144
  8.5 0.0 copy-done.2
  8.6 1.1 %fusion.17 = (bf16[1,128,1,512]{3,2,1,0:T(2,128)(2,1)}, bf16[1,128,1,512]{3,2,1,0:T(2,128)(2,1)S(1)}) fusion(bf16[1,128,2,512]{3,2,1,0:T(2,128)(2,1)S(1)} %copy-done.2), kind=kLoop, calls=%fused_computation.29 | loop fusion | bytes 524288 | tf_op jit(solution)/shard_map/slice | solution.py:499
  9.6 1.1 %copy.57 = bf16[1,128,1,512]{1,3,2,0:T(8,128)(2,1)S(1)} copy(bf16[1,128,1,512]{3,2,1,0:T(2,128)(2,1)} %get-tuple-element.14) | data formatting | bytes 262144
  10.7 1.0 fusion.6
  11.8 1.8 %copy.44 = bf16[64,8,2,512]{3,0,2,1:T(8,128)(2,1)S(1)} copy(bf16[64,8,2,512]{3,2,1,0:T(2,128)(2,1)} %param.12) | data formatting | bytes 2097152 | tf_op args[2]
  13.6 0.8 convolution_bitcast_fusion.1.kv_ref
  14.4 0.0 copy-done
  14.4 4.8 %convolution_bitcast_fusion.x_ref = f32[4,64,4096]{2,1,0:T(8,128)} fusion(bf16[64,4,4096]{2,1,0:T(4,128)(2,1)S(1)} %copy-done, s32[64]{0:T(128)S(1)} %multiply_add_fusion), kind=kOutput, calls=%fused_computation | convolution fusion | flops 134221824 | bytes 6291712 | tf_op jit(solution)/shard_map/pr,rse->spe/dot_general | solution.py:509
  19.1 71.7 %shard_map.113 = (f32[4,64,4096]{2,1,0:T(8,128)}, f32[8,8,128]{2,1,0:T(8,128)S(1)}) custom-call(bf16[528,512]{1,0:T(8,128)(2,1)S(1)} %constant_dynamic-update-slice_fusion.blk_ref, f32[4,64,4096]{2,1,0:T(8,128)} %convolution_bitcast_fusion.x_ref, f32[12,2,64,512]{3,2,1,0:T(8,128)S(1)} %convolution_bitcast_fusion.1.kv_ref, ...), custom_call_target="tpu_custom_call" | custom-call | tf_op jit(solution)/shard_map/pallas_call | solution.py:524
  90.8 2.9 %convolution_convert_fusion = bf16[64,4,4096]{2,0,1:T(8,128)(2,1)S(1)} fusion(f32[4,64,4096]{2,1,0:T(8,128)} %get-tuple-element.4, s32[64]{0:T(128)S(1)} %multiply_add_fusion), kind=kOutput, calls=%fused_computation.1 | convolution fusion | flops 136318976 | bytes 6291712 | tf_op jit(solution)/shard_map/pr,spe->rse/dot_general | solution.py:555
  93.7 2.9 %copy.49 = bf16[64,4,4096]{2,1,0:T(4,128)(2,1)} copy(bf16[64,4,4096]{2,0,1:T(8,128)(2,1)S(1)} %convolution_convert_fusion) | data formatting | bytes 4194304
  96.7 0.2 reshape.40
  96.9 0.7 reshape.41
  (11 shorter events, 0.1 us)
Async XLA Ops:
  0.6 13.8 %copy-start = (bf16[64,4,4096]{2,1,0:T(4,128)(2,1)S(1)}, bf16[64,4,4096]{2,1,0:T(4,128)(2,1)}, u32[]{:S(2)}) copy-start(bf16[64,4,4096]{2,1,0:T(4,128)(2,1)} %param.10) | copy-start | bytes 6291460
  0.6 7.9 %copy-start.2 = (bf16[1,128,2,512]{3,2,1,0:T(2,128)(2,1)S(1)}, bf16[1,128,2,512]{3,2,1,0:T(2,128)(2,1)}, u32[]{:S(2)}) copy-start(bf16[1,128,2,512]{3,2,1,0:T(2,128)(2,1)} %param.14) | copy-start | bytes 786436
  0.7 5.6 %copy-start.1 = (bf16[1,128,2,512]{3,2,1,0:T(2,128)(2,1)S(1)}, bf16[1,128,2,512]{3,2,1,0:T(2,128)(2,1)}, u32[]{:S(2)}) copy-start(bf16[1,128,2,512]{3,2,1,0:T(2,128)(2,1)} %param.13) | copy-start | bytes 786436

commit v3 on v2

--- a/solution.py
+++ b/solution.py
@@ -224,7 +224,7 @@
     prompt_valid = k_iota.astype(jnp.float32) < prompt_len
     same_row = lax.rem(q_iota, rows) == lax.rem(k_iota, rows)
     key_t = lax.div(k_iota, rows)
-    cached = same_row & (key_t < resp_slots) & (key_t < lens)
+    cached = same_row & (key_t < resp_slots) & (key_t.astype(jnp.float32) < lens)
     fresh = same_row & (key_t >= resp_slots)
     first = (q_iota < lanes // 2).astype(jnp.float32)
     second = (1.0 - first).astype(jnp.bfloat16)
@@ -289,20 +289,52 @@
         put_score(s, score)
 
 
+def place_rows(dims, owners, row_ref, lane_scr):
+    rows, _, _, _, _, group = dims
+    owner = row_ref[0:1, :]
+    count = owner.shape[1]
+    sub = lax.broadcasted_iota(jnp.int32, (count, count), 0)
+    lane = lax.broadcasted_iota(jnp.int32, (count, count), 1)
+
+    def column(row):
+        return jnp.sum(jnp.where(sub == lane, row, 0), axis=1, keepdims=True)
+
+    same = (column(owner) == owner) & (sub < lane)
+    rank = jnp.sum(jnp.where(same, 1, 0), axis=0, keepdims=True)
+    slot = owner * rows + rank
+    row_at = jnp.where(sub == slot, 1.0, 0.0).astype(jnp.bfloat16)
+    slot_at = jnp.where(column(slot) == lane, 1.0, 0.0).astype(jnp.bfloat16)
+    lanes = 2 * group * rows
+    of_lane = lax.rem(lax.broadcasted_iota(jnp.int32, (count, lanes), 1), rows)
+    spread = jnp.where(column(rank) == of_lane, 1.0, 0.0).astype(jnp.bfloat16)
+    owner_id = lax.broadcasted_iota(jnp.int32, (owners, count), 0)
+    for i in range(2):
+        value = row_ref[i + 1 : i + 2, :].astype(jnp.float32)
+        mine = jnp.where(owner_id == owner, value, 0.0).astype(jnp.bfloat16)
+        lane_scr[i] = dot_n(mine, spread)
+    return row_at, slot_at
+
+
 def fused_kernel(
     dims,
-    blk_ref,
+    pol_ref,
+    ref_ref,
+    plen_ref,
     x_ref,
-    kv_ref,
-    len_ref,
-    done_ref,
+    cache_ref,
+    new_ref,
+    row_ref,
     probe_ref,
     dec_ref,
     score_ref,
     buf,
+    x_scr,
+    kv_scr,
+    dec_scr,
+    lane_scr,
+    probe_scr,
     mail,
     got,
-    own_sem,
     send_sem,
     recv_sem,
     mail_send,
@@ -352,10 +384,35 @@
         pl.when((z > 0) & (zz >= z))(lambda: act(o, 1))
         act(o, 2)
 
-    each_way(z, lambda o, way: hop(blk_ref, o, way).start())
-    own = pltpu.make_async_copy(blk_ref, buf.at[me], own_sem)
-    own.start()
-    own.wait()
+    for i, prompt_ref in enumerate((pol_ref, ref_ref)):
+        top = 2 * i * width
+        buf[me, top : top + width, :] = prompt_ref[0]
+        for k in range(kv_heads):
+            cols = slice(k * HD, (k + 1) * HD)
+            turned = prompt_ref[1, :, cols].astype(jnp.float32).T
+            buf[me, top + width : top + 2 * width, cols] = turned.astype(jnp.bfloat16)
+    plen = jnp.broadcast_to(plen_ref[0:1, :].astype(jnp.float32), (16, HD))
+    for k in range(kv_heads):
+        buf[me, 4 * width :, k * HD : (k + 1) * HD] = plen.astype(jnp.bfloat16)
+    each_way(z, lambda o, way: hop(buf.at[o], o, way).start())
+    row_at, slot_at = place_rows(dims, n, row_ref, lane_scr)
+    pairs = kv_heads // 2
+    for p in range(pairs):
+        by_head = probe_ref[2 * p * group : 2 * (p + 1) * group]
+        spread = jnp.concatenate(
+            [jnp.broadcast_to(by_head[i : i + 1], (rows, HD)) for i in range(2 * group)], axis=0
+        )
+        probe_scr[p] = spread.T
+    for t in range(resp_slots + step_count):
+        for c in range(2):
+            held = cache_ref[t, c] if t < resp_slots else new_ref[t - resp_slots, c]
+            kv_scr[t, c] = dot_n(row_at, held)
+
+    def place_x(s, carry):
+        x_scr[s] = dot_n(row_at, x_ref[s])
+        return carry
+
+    lax.fori_loop(0, step_count, place_x, 0)
 
     def by_distance(i):
         up, down = half - 1 - z, z
@@ -397,19 +454,19 @@
         def put_decoded(s, p, decoded):
             for i in range(2 * group):
                 h = 2 * p * group + i
-                dec_ref[s, here, h * HD : (h + 1) * HD] = decoded[i * rows : (i + 1) * rows]
+                dec_scr[s, here, h * HD : (h + 1) * HD] = decoded[i * rows : (i + 1) * rows]
 
         def put_score(s, score):
-            mail[o, s : s + 1, :] = jnp.where(done_ref[o, 0:1, :] == 1, score, 0.0)
+            mail[o, s : s + 1, :] = jnp.where(lane_scr[1, pl.ds(o, 1), :] > 0.5, score, 0.0)
 
         owner_block(
             dims,
             lambda i: buf[o, i * width : (i + 1) * width, :],
             buf[o, 4 * width :, :HD][0:1].astype(jnp.float32),
-            lambda s, h: x_ref[s, here, h * HD : (h + 1) * HD],
-            lambda t, c, k: kv_ref[t, c, here, k * HD : (k + 1) * HD],
-            len_ref[o, 0:1, :],
-            lambda p: probe_ref[p],
+            lambda s, h: x_scr[s, here, h * HD : (h + 1) * HD],
+            lambda t, c, k: kv_scr[t, c, here, k * HD : (k + 1) * HD],
+            lane_scr[0, pl.ds(o, 1), :],
+            lambda p: probe_scr[p],
             put_decoded,
             put_score,
         )
@@ -425,6 +482,12 @@
 
     mail[...] = jnp.zeros_like(mail)
     lax.fori_loop(0, n, turn, 0)
+
+    def place_decoded(s, carry):
+        dec_ref[s] = dot_n(slot_at, dec_scr[s].astype(jnp.bfloat16)).astype(jnp.bfloat16)
+        return carry
+
+    lax.fori_loop(0, step_count, place_decoded, 0)
 
     def arrived(t, b):
         return pltpu.make_async_remote_copy(
@@ -486,54 +549,27 @@
     width = policy_prompt.shape[1]
     lanes = 2 * group * capacity
     pairs = kv_heads // 2
-
-    def turned(values):
-        by_head = values.reshape(width, kv_heads, HD)
-        return jnp.transpose(by_head, (2, 1, 0)).reshape(HD, kv_heads * width)
-
-    block = jnp.concatenate(
-        [
-            policy_prompt[0, :, 0],
-            turned(policy_prompt[0, :, 1]),
-            ref_prompt[0, :, 0],
-            turned(ref_prompt[0, :, 1]),
-            jnp.broadcast_to(prompt_len.astype(jnp.bfloat16)[None, :], (16, kv_width)),
-        ],
-        axis=0,
-    )
-    iota = jnp.arange(row_count, dtype=jnp.int32)
-    earlier = (row_owner[:, None] == row_owner[None, :]) & (iota[None, :] < iota[:, None])
-    slot_index = row_owner * capacity + jnp.sum(earlier.astype(jnp.int32), axis=1)
-    place = slot_index[None, :] == jnp.arange(slots, dtype=jnp.int32)[:, None]
-    one_hot = place.astype(jnp.bfloat16)
-    x_slots = jnp.einsum("pr,rse->spe", one_hot, step_input, preferred_element_type=jnp.float32)
-    own_all = jnp.concatenate([resp_cache, new_kv], axis=1)
-    kv_slots = jnp.einsum("pr,rtce->tcpe", one_hot, own_all, preferred_element_type=jnp.float32)
-    len_slots = jnp.sum(jnp.where(place, resp_len[None, :], 0), axis=1)
-    done_slots = jnp.sum(jnp.where(place, finished[None, :], 0), axis=1)
     dims = (capacity, step_count, resp_slots, width, kv_heads, group)
-
-    def on_lanes(values):
-        by_slot = values.reshape(peers, 1, 1, capacity)
-        return jnp.broadcast_to(by_slot, (peers, 8, 2 * group, capacity)).reshape(
-            peers, 8, lanes
-        )
 
     tensors = lax.axis_size("tensor")
     vmem = pl.BlockSpec(memory_space=pltpu.VMEM)
     decoded, scores = pl.pallas_call(
         functools.partial(fused_kernel, dims),
-        in_specs=[vmem] * 6,
+        in_specs=[vmem] * 8,
         out_specs=[vmem] * 2,
         out_shape=[
-            jax.ShapeDtypeStruct((step_count, slots, q_width), jnp.float32),
+            jax.ShapeDtypeStruct((step_count, row_count, q_width), jnp.bfloat16),
             jax.ShapeDtypeStruct((peers, 8, lanes), jnp.float32),
         ],
         scratch_shapes=[
-            pltpu.VMEM((peers,) + block.shape, jnp.bfloat16),
+            pltpu.VMEM((peers, 4 * width + 16, kv_width), jnp.bfloat16),
+            pltpu.VMEM((step_count, slots, q_width), jnp.float32),
+            pltpu.VMEM((keys_n, 2, slots, kv_width), jnp.float32),
+            pltpu.VMEM((step_count, slots, q_width), jnp.float32),
+            pltpu.VMEM((2, peers, lanes), jnp.float32),
+            pltpu.VMEM((pairs, HD, lanes), jnp.float32),
             pltpu.VMEM((peers, 8, lanes), jnp.float32),
             pltpu.VMEM((tensors, peers, 8, lanes), jnp.float32),
-            pltpu.SemaphoreType.DMA,
             pltpu.SemaphoreType.DMA((3, peers)),
             pltpu.SemaphoreType.DMA((peers,)),
             pltpu.SemaphoreType.DMA((tensors, peers)),
@@ -543,21 +579,16 @@
             collective_id=0, has_side_effects=True, vmem_limit_bytes=48 * 1024 * 1024
         ),
     )(
-        block,
-        x_slots,
-        kv_slots,
-        on_lanes(len_slots),
-        on_lanes(done_slots),
-        jnp.repeat(
-            jnp.transpose(probe.reshape(pairs, 2 * group, HD), (0, 2, 1)), capacity, axis=2
-        ),
+        jnp.transpose(policy_prompt[0], (1, 0, 2)),
+        jnp.transpose(ref_prompt[0], (1, 0, 2)),
+        jnp.broadcast_to(prompt_len[:, None], (8, HD)),
+        jnp.transpose(step_input, (1, 0, 2)),
+        jnp.transpose(resp_cache, (1, 2, 0, 3)),
+        jnp.transpose(new_kv, (1, 2, 0, 3)),
+        jnp.stack([row_owner, resp_len, finished] + [finished] * 5),
+        probe.reshape(q_heads, HD),
     )
-    decoded_rows = jnp.einsum(
-        "pr,spe->rse",
-        one_hot,
-        decoded.astype(jnp.bfloat16),
-        preferred_element_type=jnp.float32,
-    ).astype(jnp.bfloat16)
+    decoded_rows = jnp.transpose(decoded, (1, 0, 2))
     scores = scores[:, :step_count].reshape(peers, step_count, 2 * group, capacity)
     scores = jnp.transpose(jnp.sum(scores, axis=2), (0, 2, 1))
     return decoded_rows, scores.reshape(1, slots, step_count)

time: 98.1 us -> 81.1 us (0.83)
  matrix products: 8.45 us -> 0 us
  local copies, waits for them, and re-layouts: 13.4 us -> 10.2 us
  Pallas kernels: 71.7 us -> 69.2 us
  other arithmetic: 2.4 us -> 0.05 us
    dot_general x3 -> x0, matrix products: 8.45 us -> none  [the longest x1 4.76 us: per_device_gathered(): jnp.einsum('pr,rse->spe', one_hot, step_input, preferred_element_type=jnp...]
    pallas_call x1, Pallas kernels: 71.7 us -> 69.2 us  [per_device_gathered(): pl.pallas_call(functools.partial(fused_kernel, dims), in_specs=[vmem] * 8...]
    slice x2 -> x0, local copies, waits for them, and re-layouts: 2.22 us -> none  [the longest x1 1.15 us: per_device_gathered(): policy_prompt[0, :, 1]]
    unnamed x15 -> x10, local copies, waits for them, and re-layouts: 9.2 us -> 7.35 us
    reduce_sum x2 -> x0, other arithmetic: 1.68 us -> none  [the longest x1 0.91 us: per_device_gathered(): jnp.sum(earlier.astype(jnp.int32), axis=1)]
    transpose x0 -> x1, local copies, waits for them, and re-layouts: none -> 1.09 us  [per_device_gathered(): jnp.transpose(ref_prompt[0], (1, 0, 2))]
where the time goes in v3:
time: 81.1 us; the launch traced here: 80.9 us
  Pallas kernels  69.2 us (85%)
  local copies, waits for them, and re-layouts  10.2 us (13%)
  between operations  1.45 us (2%)
    pallas_call x1, Pallas kernels, per_device_gathered(): pl.pallas_call(functools.partial(fused_kernel, dims), in_specs=[vmem] * 8...  69.2 us
    unnamed x10, local copies, waits for them, and re-layouts  7.35 us

profile of v3, /device:TPU:0, one launch (start us, length us, event | category | flops | bytes accessed | tf_op | source)
XLA Modules:
  0.0 80.9 jit_solution(9613580422246903246)
XLA Ops:
  0.6 0.0 copy-start.2
  1.4 0.9 %stack.20.row_ref = s32[8,64]{1,0:T(8,128)S(1)} concatenate(s32[1,64]{1,0:T(1,128)} %bitcast.41, s32[1,64]{1,0:T(1,128)} %bitcast.42, s32[1,64]{1,0:T(1,128)} %bitcast.35, s32[1,64]{1,0:T(1,128)} %bitcast.36, s32[1,64]{1,0:T(1,128)} %bitcast.37, s32[1,64]{1,0:T(1,128)} %bitcast.38, s32[1,64]{1,0:T(1,128)} %bitcast.39, s32[1,64]{1,0:T(1,128)} %bitcast.40), dimensions={0} | concatenate | bytes 4096 | tf_op jit(solution)/shard_map/stack | solution.py:588
  2.3 0.0 copy-start.1
  2.3 1.3 %copy.32 = bf16[64,4,2,512]{3,0,2,1:T(8,128)(2,1)S(1)} copy(bf16[64,4,2,512]{3,2,1,0:T(2,128)(2,1)} %param.11) | data formatting | bytes 1048576 | tf_op args[1]
  3.6 1.1 %copy_bitcast_fusion.3 = (bf16[2,128,512]{2,1,0:T(8,128)(2,1)S(1)}, bf16[2,128,512]{2,1,0:T(8,128)(2,1)S(1)}) fusion(bf16[1,128,2,512]{3,2,1,0:T(2,128)(2,1)} %param.14, bf16[1,128,2,512]{3,2,1,0:T(2,128)(2,1)} %param.13), kind=kLoop, calls=%fused_computation.3 | loop fusion | bytes 1048576 | tf_op jit(solution)/shard_map/transpose | solution.py:583
  4.7 0.0 copy-done.2
  4.7 0.6 copy.31
  5.3 0.0 copy-done.1
  5.3 0.0 copy-start
  5.4 2.5 %copy.30 = bf16[64,4,4096]{2,0,1:T(8,128)(2,1)} copy(bf16[64,4,4096]{2,1,0:T(4,128)(2,1)S(1)} %copy-done.1) | data formatting | bytes 4194304 | tf_op args[0]
  7.8 0.0 copy-done
  7.8 69.2 %shard_map.113 = (bf16[4,64,4096]{2,1,0:T(8,128)(2,1)S(1)}, f32[8,8,128]{2,1,0:T(8,128)S(1)}) custom-call(bf16[2,128,512]{2,1,0:T(8,128)(2,1)S(1)} %get-tuple-element.11.pol_ref, bf16[2,128,512]{2,1,0:T(8,128)(2,1)S(1)} %get-tuple-element.10.ref_ref, s32[8,128]{1,0:T(8,128)S(1)} %broadcast_in_dim.9.plen_ref, bf16[4,64,4096]{2,1,0:T(8,128)(2,1)} %bitcast.33, ...), custom_call_target="tpu_custom_call" | custom-call | tf_op jit(solution)/shard_map/pallas_call | solution.py:556
  77.1 2.9 %copy.24 = bf16[64,4,4096]{2,1,0:T(4,128)(2,1)} copy(bf16[64,4,4096]{2,0,1:T(8,128)(2,1)S(1)} %bitcast.30) | data formatting | bytes 4194304
  80.0 0.2 reshape.15
  80.2 0.7 reshape.16
  (4 shorter events, 0.1 us)
Async XLA Ops:
  0.6 4.1 %copy-start.2 = (bf16[64,8,2,512]{3,2,1,0:T(2,128)(2,1)S(1)}, bf16[64,8,2,512]{3,2,1,0:T(2,128)(2,1)}, u32[]{:S(2)}) copy-start(bf16[64,8,2,512]{3,2,1,0:T(2,128)(2,1)} %param.12) | copy-start | bytes 3145732
  2.3 3.1 %copy-start.1 = (bf16[64,4,4096]{2,1,0:T(4,128)(2,1)S(1)}, bf16[64,4,4096]{2,1,0:T(4,128)(2,1)}, u32[]{:S(2)}) copy-start(bf16[64,4,4096]{2,1,0:T(4,128)(2,1)} %param.10) | copy-start | bytes 6291460
  5.3 2.5 %copy-start = (f32[4096]{0:T(1024)S(1)}, f32[4096]{0:T(1024)}, u32[]{:S(2)}) copy-start(f32[4096]{0:T(1024)} %param.19) | copy-start | bytes 49156

commit v4 on v3

--- a/solution.py
+++ b/solution.py
@@ -337,6 +337,8 @@
     got,
     send_sem,
     recv_sem,
+    tail_send,
+    tail_recv,
     mail_send,
     mail_recv,
 ):
@@ -378,11 +380,37 @@
             device_id_type=pl.DeviceIdType.MESH,
         )
 
-    def each_way(zz, act):
+    next_z = z + 1 - 2 * lax.rem(z, 2)
+    cut = 2 * width
+
+    def short_hop(o):
+        head = buf.at[o, pl.ds(0, cut)]
+        return pltpu.make_async_remote_copy(
+            src_ref=head,
+            dst_ref=head,
+            send_sem=send_sem.at[2, o],
+            recv_sem=recv_sem.at[o],
+            device_id=device(across, tau),
+            device_id_type=pl.DeviceIdType.MESH,
+        )
+
+    def tail_hop(o):
+        tail = buf.at[o, pl.ds(cut, buf.shape[1] - cut)]
+        return pltpu.make_async_remote_copy(
+            src_ref=tail,
+            dst_ref=tail,
+            send_sem=tail_send,
+            recv_sem=tail_recv,
+            device_id=device(2 * next_z + y, tau),
+            device_id_type=pl.DeviceIdType.MESH,
+        )
+
+    def each_way(zz, act, act_short):
         o = 2 * zz + y
         pl.when((z < half - 1) & (zz <= z))(lambda: act(o, 0))
         pl.when((z > 0) & (zz >= z))(lambda: act(o, 1))
-        act(o, 2)
+        pl.when(zz == next_z)(lambda: act_short(o))
+        pl.when(zz != next_z)(lambda: act(o, 2))
 
     for i, prompt_ref in enumerate((pol_ref, ref_ref)):
         top = 2 * i * width
@@ -394,7 +422,7 @@
     plen = jnp.broadcast_to(plen_ref[0:1, :].astype(jnp.float32), (16, HD))
     for k in range(kv_heads):
         buf[me, 4 * width :, k * HD : (k + 1) * HD] = plen.astype(jnp.bfloat16)
-    each_way(z, lambda o, way: hop(buf.at[o], o, way).start())
+    each_way(z, lambda o, way: hop(buf.at[o], o, way).start(), lambda o: short_hop(o).start())
     row_at, slot_at = place_rows(dims, n, row_ref, lane_scr)
     pairs = kv_heads // 2
     for p in range(pairs):
@@ -441,13 +469,28 @@
         zz = by_distance(order)
         o = 2 * zz + jnp.where(line, y, 1 - y)
 
-        @pl.when(t > 0)
+        in_two = jnp.logical_not(line) & (zz == next_z)
+
+        @pl.when((t > 0) & jnp.logical_not(in_two))
         def _():
             hop(buf.at[o], o, 2).wait_recv()
 
+        @pl.when(in_two)
+        def _():
+            short_hop(o).wait_recv()
+            tail_hop(o).wait_recv()
+
         @pl.when((t > 0) & line)
         def _():
-            each_way(zz, lambda b, way: hop(buf.at[b], b, way).start())
+            each_way(
+                zz,
+                lambda b, way: hop(buf.at[b], b, way).start(),
+                lambda b: short_hop(b).start(),
+            )
+
+        @pl.when(jnp.logical_not(line) & (zz == z))
+        def _():
+            tail_hop(o).start()
 
         here = pl.ds(pl.multiple_of(o * rows, rows), rows)
 
@@ -514,10 +557,15 @@
     lax.fori_loop(0, n, finish, 0)
 
     def sent(zz, carry):
-        each_way(zz, lambda o, way: hop(buf.at[o], o, way).wait_send())
+        each_way(
+            zz,
+            lambda o, way: hop(buf.at[o], o, way).wait_send(),
+            lambda o: short_hop(o).wait_send(),
+        )
         return carry
 
     lax.fori_loop(0, half, sent, 0)
+    tail_hop(across).wait_send()
     total = got[0]
     for t in range(1, tensors):
         total = total + got[t]
@@ -572,6 +620,8 @@
             pltpu.VMEM((tensors, peers, 8, lanes), jnp.float32),
             pltpu.SemaphoreType.DMA((3, peers)),
             pltpu.SemaphoreType.DMA((peers,)),
+            pltpu.SemaphoreType.DMA,
+            pltpu.SemaphoreType.DMA,
             pltpu.SemaphoreType.DMA((tensors, peers)),
             pltpu.SemaphoreType.DMA((tensors, peers)),
         ],
@@ -605,7 +655,7 @@
         and 16 * q_width == HD * kv_width
         and kv_width % (2 * HD) == 0
         and 8 * (resp_slots + step_count) <= HD
-        and peers % 2 == 0
+        and peers % 4 == 0
         and step_count <= 8
     )
     if fits:

time: 81.1 us -> 84.6 us (1.043)
  Pallas kernels: 69.2 us -> 72.7 us
    pallas_call x1, Pallas kernels: 69.2 us -> 72.7 us  [per_device_gathered(): pl.pallas_call(functools.partial(fused_kernel, dims), in_specs=[vmem] * 8...]
where the time goes in v4:
time: 84.6 us; the launch traced here: 84.4 us
  Pallas kernels  72.7 us (86%)
  local copies, waits for them, and re-layouts  10.2 us (12%)
  between operations  1.45 us (2%)
    pallas_call x1, Pallas kernels, per_device_gathered(): pl.pallas_call(functools.partial(fused_kernel, dims), in_specs=[vmem] * 8...  72.7 us
    unnamed x10, local copies, waits for them, and re-layouts  7.35 us

profile of v4, /device:TPU:0, one launch (start us, length us, event | category | flops | bytes accessed | tf_op | source)
XLA Modules:
  0.0 84.4 jit_solution(16402547926760134766)
XLA Ops:
  0.6 0.0 copy-start.2
  1.4 0.9 %stack.20.row_ref = s32[8,64]{1,0:T(8,128)S(1)} concatenate(s32[1,64]{1,0:T(1,128)} %bitcast.41, s32[1,64]{1,0:T(1,128)} %bitcast.42, s32[1,64]{1,0:T(1,128)} %bitcast.35, s32[1,64]{1,0:T(1,128)} %bitcast.36, s32[1,64]{1,0:T(1,128)} %bitcast.37, s32[1,64]{1,0:T(1,128)} %bitcast.38, s32[1,64]{1,0:T(1,128)} %bitcast.39, s32[1,64]{1,0:T(1,128)} %bitcast.40), dimensions={0} | concatenate | bytes 4096 | tf_op jit(solution)/shard_map/stack | solution.py:638
  2.3 0.0 copy-start.1
  2.3 1.3 %copy.32 = bf16[64,4,2,512]{3,0,2,1:T(8,128)(2,1)S(1)} copy(bf16[64,4,2,512]{3,2,1,0:T(2,128)(2,1)} %param.11) | data formatting | bytes 1048576 | tf_op args[1]
  3.6 1.1 %copy_bitcast_fusion.3 = (bf16[2,128,512]{2,1,0:T(8,128)(2,1)S(1)}, bf16[2,128,512]{2,1,0:T(8,128)(2,1)S(1)}) fusion(bf16[1,128,2,512]{3,2,1,0:T(2,128)(2,1)} %param.14, bf16[1,128,2,512]{3,2,1,0:T(2,128)(2,1)} %param.13), kind=kLoop, calls=%fused_computation.3 | loop fusion | bytes 1048576 | tf_op jit(solution)/shard_map/transpose | solution.py:633
  4.7 0.0 copy-done.2
  4.7 0.6 copy.31
  5.3 0.0 copy-done.1
  5.3 0.0 copy-start
  5.4 2.5 %copy.30 = bf16[64,4,4096]{2,0,1:T(8,128)(2,1)} copy(bf16[64,4,4096]{2,1,0:T(4,128)(2,1)S(1)} %copy-done.1) | data formatting | bytes 4194304 | tf_op args[0]
  7.8 0.0 copy-done
  7.8 72.7 %shard_map.113 = (bf16[4,64,4096]{2,1,0:T(8,128)(2,1)S(1)}, f32[8,8,128]{2,1,0:T(8,128)S(1)}) custom-call(bf16[2,128,512]{2,1,0:T(8,128)(2,1)S(1)} %get-tuple-element.11.pol_ref, bf16[2,128,512]{2,1,0:T(8,128)(2,1)S(1)} %get-tuple-element.10.ref_ref, s32[8,128]{1,0:T(8,128)S(1)} %broadcast_in_dim.9.plen_ref, bf16[4,64,4096]{2,1,0:T(8,128)(2,1)} %bitcast.33, ...), custom_call_target="tpu_custom_call" | custom-call | tf_op jit(solution)/shard_map/pallas_call | solution.py:604
  80.6 2.9 %copy.24 = bf16[64,4,4096]{2,1,0:T(4,128)(2,1)} copy(bf16[64,4,4096]{2,0,1:T(8,128)(2,1)S(1)} %bitcast.30) | data formatting | bytes 4194304
  83.5 0.2 reshape.15
  83.7 0.7 reshape.16
  (4 shorter events, 0.1 us)
Async XLA Ops:
  0.6 4.1 %copy-start.2 = (bf16[64,8,2,512]{3,2,1,0:T(2,128)(2,1)S(1)}, bf16[64,8,2,512]{3,2,1,0:T(2,128)(2,1)}, u32[]{:S(2)}) copy-start(bf16[64,8,2,512]{3,2,1,0:T(2,128)(2,1)} %param.12) | copy-start | bytes 3145732
  2.3 3.1 %copy-start.1 = (bf16[64,4,4096]{2,1,0:T(4,128)(2,1)S(1)}, bf16[64,4,4096]{2,1,0:T(4,128)(2,1)}, u32[]{:S(2)}) copy-start(bf16[64,4,4096]{2,1,0:T(4,128)(2,1)} %param.10) | copy-start | bytes 6291460
  5.3 2.5 %copy-start = (f32[4096]{0:T(1024)S(1)}, f32[4096]{0:T(1024)}, u32[]{:S(2)}) copy-start(f32[4096]{0:T(1024)} %param.19) | copy-start | bytes 49156
